TPU v7x, 32 devices: a whole 2x2x4 slice. The times are simulated.
32 devices in a mesh: groups: 2 (over x), seq: 16 (over z, y, core).
Axes of the slice: x: 2, y: 2, z: 4, core: 2. Of those that a mesh axis runs over, the one named last changes fastest.
Arguments:
- queries: bfloat16 [24576, 1024], P(('groups', 'seq')), parts along dimension 0, may hold values from -4 to 4
- resp_keys: bfloat16 [24576, 128], P(('groups', 'seq')), parts along dimension 0, may hold values from -6 to 6
- resp_values: bfloat16 [24576, 128], P(('groups', 'seq')), parts along dimension 0, may hold values from -6 to 6
- out_grad: bfloat16 [24576, 1024], P(('groups', 'seq')), parts along dimension 0, may hold values from -48 to 48
- prompt_keys: bfloat16 [1024, 128], P(('groups', 'seq')), parts along dimension 0, may hold values from -7.5 to 7.5
- prompt_values: bfloat16 [1024, 128], P(('groups', 'seq')), parts along dimension 0, may hold values from -6 to 6
- slot_prompt: int32 [64], P(('groups', 'seq')), parts along dimension 0, may hold values from 0 to 1, as said below
- slot_length: int32 [64], P(('groups', 'seq')), parts along dimension 0, may hold values from 76 to 384
- slot_begin: int32 [64], P(('groups', 'seq')), parts along dimension 0, may hold values from 0 to 308, as said below
- block_prompt: int32 [32], P('groups'), parts along dimension 0, may hold values from 0 to 15, as said below
Outputs:
- query_grad: float32 [24576, 1024], P(('groups', 'seq')), parts along dimension 0
- resp_key_grad: float32 [24576, 128], P(('groups', 'seq')), parts along dimension 0
- resp_value_grad: float32 [24576, 128], P(('groups', 'seq')), parts along dimension 0
- prompt_key_grad: float32 [1024, 128], P(('groups', 'seq')), parts along dimension 0
- prompt_value_grad: float32 [1024, 128], P(('groups', 'seq')), parts along dimension 0
There are 2 independent parts, one for each index of `groups`. A program takes and returns all parts, laid end to end along the dimension named above; each array names one. Nothing has to cross between parts.
Inputs may be any that keep to these rules, and one draw needn't show every extreme that they name: `slot_prompt`: each prompt number is named by exactly 16 slots. slot_begin + slot_length <= 384 for every slot. `block_prompt`: a permutation: each value names one piece of one prompt.
All inputs are finite; a program needn't handle non-finite values.
Results may differ from a plain program's by a relative error of at most 0.012.
The roundings to bfloat16 on the way count: a program that leaves them out, or rounds other values in their place, can miss the bound.
Values may be sent and summed in bfloat16 or wider, within the bound.
No kernel may reach another device: no remote copies, remote signals or barrier semaphores. Data moves between devices by JAX's collectives and lax.ppermute only.
A program may use at most 128 MiB of HBM per device.

v0:
```python
import functools
import math

import jax
import jax.numpy as jnp
from jax import lax
from jax.experimental import pallas as pl
from jax.experimental.pallas import tpu as pltpu
from jax.sharding import PartitionSpec as P

OWNERS = 8
TILE = 128
PIECE = 16
score_scale = 0.08838834764831845
EXP2_SCALE = score_scale * math.log2(math.e)
MASKED = -1e30


def same_core_groups(n):
    return [list(range(core, n, 2)) for core in range(2)]


def swap_cores(x, n):
    return lax.ppermute(x, "seq", [(i, i ^ 1) for i in range(n)])


def exchange(x, n):
    return lax.all_to_all(
        x, "seq", split_axis=0, concat_axis=0, axis_index_groups=same_core_groups(n), tiled=True
    )


def block_position(holder, me, n):
    return ((holder ^ me) & 1) * (n // 2) + (holder >> 1)


def grad_kernel(
    prompt_hbm,
    length_hbm,
    begin_hbm,
    holder_hbm,
    q_hbm,
    g_hbm,
    rk_hbm,
    rv_hbm,
    own_hbm,
    other_hbm,
    dq_hbm,
    drk_hbm,
    drv_hbm,
    own_term_hbm,
    other_term_hbm,
    prompt_ref,
    length_ref,
    begin_ref,
    holder_ref,
    place,
    q_all,
    g_all,
    rk_all,
    rv_all,
    dq_all,
    drk_all,
    drv_all,
    kv,
    term_ref,
    keys,
    values,
    keys_t,
    live_bias,
    causal_bias,
    turned,
    exps,
    dprobs,
    prob16,
    dscore16,
    kt,
    vt,
    sem_scalar,
    sem_resp,
    sem_q,
    sem_g,
    sem_dq,
    sem_drk,
    sem_drv,
    sem_kv,
    sem_term,
):
    n = holder_ref.shape[0]
    slots = prompt_ref.shape[0]
    rows, width = rk_all.shape
    slot_rows = rows // slots
    tiles = slot_rows // TILE
    prow = term_ref.shape[0] // n
    prompt_len = prow * OWNERS
    heads = q_all.shape[1] // width
    me = lax.axis_index("seq")

    scalar_copies = [
        pltpu.make_async_copy(src, dst, sem_scalar.at[i])
        for i, (src, dst) in enumerate(
            [
                (prompt_hbm, prompt_ref),
                (length_hbm, length_ref),
                (begin_hbm, begin_ref),
                (holder_hbm, holder_ref),
            ]
        )
    ]
    resp_copies = [
        pltpu.make_async_copy(rk_hbm, rk_all, sem_resp.at[0]),
        pltpu.make_async_copy(rv_hbm, rv_all, sem_resp.at[1]),
    ]

    def tile_rows(chunk):
        return pl.ds(pl.multiple_of(chunk * TILE, TILE), TILE)

    def q_copy(chunk):
        part = tile_rows(chunk)
        return pltpu.make_async_copy(q_hbm.at[part], q_all.at[part], sem_q.at[chunk])

    def g_copy(chunk):
        part = tile_rows(chunk)
        return pltpu.make_async_copy(g_hbm.at[part], g_all.at[part], sem_g.at[chunk])

    def dq_copy(chunk):
        part = tile_rows(chunk)
        return pltpu.make_async_copy(dq_all.at[part], dq_hbm.at[part], sem_dq.at[chunk])

    def slot_part(s):
        return pl.ds(pl.multiple_of(s * slot_rows, slot_rows), slot_rows)

    def drk_copy(s):
        return pltpu.make_async_copy(
            drk_all.at[slot_part(s)], drk_hbm.at[slot_part(s)], sem_drk.at[s]
        )

    def drv_copy(s):
        return pltpu.make_async_copy(
            drv_all.at[slot_part(s)], drv_hbm.at[slot_part(s)], sem_drv.at[s]
        )

    half_rows = term_ref.shape[0] // 2
    kv_copies = [
        pltpu.make_async_copy(src, kv.at[pl.ds(i * half_rows, half_rows)], sem_kv.at[i])
        for i, src in enumerate([own_hbm, other_hbm])
    ]
    term_copies = [
        pltpu.make_async_copy(term_ref.at[pl.ds(i * half_rows, half_rows)], dst, sem_term.at[i])
        for i, dst in enumerate([own_term_hbm, other_term_hbm])
    ]
    for copy in scalar_copies + kv_copies + resp_copies:
        copy.start()
    for chunk in range(slots * tiles):
        q_copy(chunk).start()
        g_copy(chunk).start()

    term_ref[...] = jnp.zeros_like(term_ref)
    causal_bias[...] = jnp.where(
        lax.broadcasted_iota(jnp.int32, (TILE, TILE), 0)
        <= lax.broadcasted_iota(jnp.int32, (TILE, TILE), 1),
        0.0,
        MASKED,
    )
    for copy in scalar_copies + kv_copies + resp_copies:
        copy.wait()

    @pl.loop(0, n)
    def _(j):
        place[holder_ref[j]] = j

    half = heads // 2
    wide = 2 * TILE
    units = [(index, pair) for index in range(tiles) for pair in range(half)]

    def columns_of(u):
        return prompt_len + (units[u][0] + 1) * TILE

    def chunks(u):
        return range(0, columns_of(u), TILE)

    def stacked(ref, s, index, first, count):
        part = tile_rows(s * tiles + index)
        return jnp.concatenate(
            [ref[part, (first + h) * width : (first + h + 1) * width] for h in range(count)], axis=0
        )

    def fold(x, how):
        return how(how(x.reshape(x.shape[0] // 8, 8, x.shape[1]), axis=0), axis=0, keepdims=True)

    def head(s, u, out):
        index, pair = units[u]
        columns, buf = columns_of(u), u % 2
        if pair == 0:
            q_copy(s * tiles + index).wait()
            g_copy(s * tiles + index).wait()
        q2t, g2t = turned.at[buf, 0], turned.at[buf, 1]
        q2t[...] = stacked(q_all, s, index, 2 * pair, 2).T
        g2t[...] = stacked(g_all, s, index, 2 * pair, 2).T
        tops, totals, weights = [], [], []
        for c in chunks(u):
            part = slice(c, c + TILE)
            block = jnp.dot(keys[part, :], q2t[...], preferred_element_type=jnp.float32)
            if c >= prompt_len:
                bias = live_bias[c - prompt_len : c - prompt_len + TILE, :]
                if c + TILE == columns:
                    bias = bias + causal_bias[...]
                block = block + jnp.concatenate([bias, bias], axis=1)
            top = fold(block, jnp.max) * EXP2_SCALE
            e = jnp.exp2(block * EXP2_SCALE - top)
            exps[buf, part, :] = e
            yield
            d = jnp.dot(values[part, :], g2t[...], preferred_element_type=jnp.float32)
            dprobs[buf, part, :] = d
            tops.append(top)
            totals.append(fold(e, jnp.sum))
            weights.append(fold(e * d, jnp.sum))
            yield
        top = functools.reduce(jnp.maximum, tops)
        factors = [jnp.exp2(part - top) for part in tops]
        total = functools.reduce(jnp.add, [f * x for f, x in zip(factors, totals)])
        weighted = functools.reduce(jnp.add, [f * x for f, x in zip(factors, weights)])
        row = index * TILE + lax.broadcasted_iota(jnp.int32, (1, TILE), 1)
        live = (row >= begin_ref[s]) & (row < begin_ref[s] + length_ref[s])
        inverse = jnp.where(jnp.concatenate([live, live], axis=1), 1.0 / total, 0.0)
        out["delta"] = weighted * inverse
        out["factors"] = [f * inverse for f in factors]

    def tail(u, stats):
        buf, group = u % 2, (u // 2) % 2
        lanes = slice((u % 2) * wide, (u % 2 + 1) * wide)
        delta = stats["delta"]
        for c, factor in zip(chunks(u), stats["factors"]):
            for first in range(c, c + TILE, PIECE):
                part = slice(first, first + PIECE)
                p = exps[buf, part, :] * factor
                prob16[group, part, lanes] = p.astype(jnp.bfloat16)
                ds = p * (dprobs[buf, part, :] - delta)
                dscore16[group, part, lanes] = ds.astype(jnp.bfloat16)
            yield

    def flush_keys(s, u):
        index, pair = units[u]
        group, columns = (u // 2) % 2, columns_of(u)
        q4 = stacked(q_all, s, index, 2 * (pair - 1), 4)
        kt[0:columns, :] += jnp.dot(
            dscore16[group, 0:columns, :], q4, preferred_element_type=jnp.float32
        )
        yield

    def flush_values(s, u):
        index, pair = units[u]
        group, columns = (u // 2) % 2, columns_of(u)
        g4 = stacked(g_all, s, index, 2 * (pair - 1), 4)
        vt[0:columns, :] += jnp.dot(
            prob16[group, 0:columns, :], g4, preferred_element_type=jnp.float32
        )
        yield

    def flush_queries(s, u):
        index, pair = units[u]
        group, columns = (u // 2) % 2, columns_of(u)
        part = tile_rows(s * tiles + index)
        for side in range(2):
            ds = dscore16[group, 0:columns, side * wide : (side + 1) * wide]
            dqt = jnp.dot(keys_t[:, 0:columns], ds, preferred_element_type=jnp.float32)
            for h in range(2):
                first = (2 * (pair - 1 + side) + h) * width
                dq_all[part, first : first + width] = dqt[:, h * TILE : (h + 1) * TILE].T * score_scale
            yield
        if pair == half - 1:
            dq_copy(s * tiles + index).start()

    def together(*steps):
        steps = list(steps)
        while steps:
            for step in list(steps):
                if next(step, steps) is steps:
                    steps.remove(step)

    def slot_units(s):
        stats = {}
        together(head(s, 0, stats))
        for u in range(len(units)):
            now, stats = stats, {}
            steps = []
            if u + 1 < len(units):
                steps.append(head(s, u + 1, stats))
            steps.append(tail(u, now))
            if u >= 2 and u % 2 == 0:
                steps += [flush_keys(s, u - 1), flush_queries(s, u - 1)]
            elif u >= 2:
                steps.append(flush_values(s, u - 2))
            together(*steps)
        last = len(units) - 1
        together(flush_keys(s, last), flush_values(s, last), flush_queries(s, last))

    @pl.loop(0, slots)
    def _(s):
        first_block = prompt_ref[s] * OWNERS
        for o in range(OWNERS):
            start = block_position(place[first_block + o], me, n) * prow
            source = pl.ds(pl.multiple_of(start, prow), prow)
            keys[o * prow : (o + 1) * prow, :] = kv[source, 0:width]
            values[o * prow : (o + 1) * prow, :] = kv[source, width : 2 * width]
        keys[prompt_len:, :] = rk_all[slot_part(s), :]
        values[prompt_len:, :] = rv_all[slot_part(s), :]
        keys_t[...] = keys[...].astype(jnp.float32).T.astype(jnp.bfloat16)
        column = lax.broadcasted_iota(jnp.int32, (slot_rows, TILE), 0)
        live_bias[...] = jnp.where(column >= begin_ref[s], 0.0, MASKED)
        kt[...] = jnp.zeros_like(kt)
        vt[...] = jnp.zeros_like(vt)
        slot_units(s)
        drk_all[slot_part(s), :] = kt[prompt_len:, :] * score_scale
        drv_all[slot_part(s), :] = vt[prompt_len:, :]
        drk_copy(s).start()
        drv_copy(s).start()
        for o in range(OWNERS):
            start = block_position(place[first_block + o], me, n) * prow
            target = pl.ds(pl.multiple_of(start, prow), prow)
            block = slice(o * prow, (o + 1) * prow)
            term_ref[target, 0:width] += kt[block, :] * score_scale
            term_ref[target, width : 2 * width] += vt[block, :]

    for copy in term_copies:
        copy.start()
    for copy in term_copies:
        copy.wait()
    for chunk in range(slots * tiles):
        dq_copy(chunk).wait()
    for s in range(slots):
        drk_copy(s).wait()
        drv_copy(s).wait()


def slot_grads(queries, resp_keys, resp_values, out_grad, own_kv, other_kv, prompts, lengths, begins, holders):
    slots = prompts.shape[0]
    rows, columns = queries.shape
    slot_rows, width = rows // slots, resp_keys.shape[1]
    n = holders.shape[0]
    prow = 2 * own_kv.shape[0] // n
    total = prow * OWNERS + slot_rows
    tiles = slot_rows // TILE
    hbm = pl.BlockSpec(memory_space=pltpu.HBM)
    f32, bf16 = jnp.float32, jnp.bfloat16
    return pl.pallas_call(
        grad_kernel,
        in_specs=[hbm] * 10,
        out_specs=[hbm] * 5,
        out_shape=[
            jax.ShapeDtypeStruct((rows, columns), f32),
            jax.ShapeDtypeStruct((rows, width), f32),
            jax.ShapeDtypeStruct((rows, width), f32),
            jax.ShapeDtypeStruct((n * prow // 2, 2 * width), f32),
            jax.ShapeDtypeStruct((n * prow // 2, 2 * width), f32),
        ],
        scratch_shapes=[
            pltpu.SMEM((slots,), jnp.int32),
            pltpu.SMEM((slots,), jnp.int32),
            pltpu.SMEM((slots,), jnp.int32),
            pltpu.SMEM((n,), jnp.int32),
            pltpu.SMEM((n,), jnp.int32),
            pltpu.VMEM((rows, columns), bf16),
            pltpu.VMEM((rows, columns), bf16),
            pltpu.VMEM((rows, width), bf16),
            pltpu.VMEM((rows, width), bf16),
            pltpu.VMEM((rows, columns), f32),
            pltpu.VMEM((rows, width), f32),
            pltpu.VMEM((rows, width), f32),
            pltpu.VMEM((n * prow, 2 * width), bf16),
            pltpu.VMEM((n * prow, 2 * width), f32),
            pltpu.VMEM((total, width), bf16),
            pltpu.VMEM((total, width), bf16),
            pltpu.VMEM((width, total), bf16),
            pltpu.VMEM((slot_rows, TILE), f32),
            pltpu.VMEM((TILE, TILE), f32),
            pltpu.VMEM((2, 2, width, 2 * TILE), bf16),
            pltpu.VMEM((2, total, 2 * TILE), f32),
            pltpu.VMEM((2, total, 2 * TILE), f32),
            pltpu.VMEM((2, total, 4 * TILE), bf16),
            pltpu.VMEM((2, total, 4 * TILE), bf16),
            pltpu.VMEM((total, width), f32),
            pltpu.VMEM((total, width), f32),
            pltpu.SemaphoreType.DMA((4,)),
            pltpu.SemaphoreType.DMA((2,)),
            pltpu.SemaphoreType.DMA((slots * tiles,)),
            pltpu.SemaphoreType.DMA((slots * tiles,)),
            pltpu.SemaphoreType.DMA((slots * tiles,)),
            pltpu.SemaphoreType.DMA((slots,)),
            pltpu.SemaphoreType.DMA((slots,)),
            pltpu.SemaphoreType.DMA((2,)),
            pltpu.SemaphoreType.DMA((2,)),
        ],
        compiler_params=pltpu.CompilerParams(vmem_limit_bytes=60 * 1024 * 1024),
    )(prompts, lengths, begins, holders, queries, out_grad, resp_keys, resp_values, own_kv, other_kv)


def body(
    n,
    queries,
    resp_keys,
    resp_values,
    out_grad,
    prompt_keys,
    prompt_values,
    slot_prompt,
    slot_length,
    slot_begin,
    block_prompt,
):
    width = resp_keys.shape[1]
    prow = prompt_keys.shape[0]
    own = jnp.pad(prompt_keys, ((0, 0), (0, width))) + jnp.pad(prompt_values, ((0, 0), (width, 0)))
    own = jnp.broadcast_to(own[None], (n // 2, prow, 2 * width)).reshape(-1, 2 * width)
    own_kv = exchange(own, n)
    other_kv = swap_cores(own_kv, n)
    query_grad, key_grad, value_grad, own_term, other_term = slot_grads(
        queries, resp_keys, resp_values, out_grad, own_kv, other_kv,
        slot_prompt, slot_length, slot_begin, block_prompt,
    )
    parts = exchange(own_term + swap_cores(other_term, n), n)
    owned = jnp.sum(parts.reshape(n // 2, prow, 2 * width), axis=0)
    return query_grad, key_grad, value_grad, owned[:, :width], owned[:, width:]


def solution(mesh):
    n = mesh.shape["seq"]
    rows = P(("groups", "seq"), None)
    slots = P(("groups", "seq"))
    return jax.shard_map(
        functools.partial(body, n),
        mesh=mesh,
        in_specs=(rows,) * 6 + (slots,) * 3 + (P("groups"),),
        out_specs=(rows,) * 5,
        check_vma=False,
    )
```

profile of v0, /device:TPU:0, one launch (start us, length us, event | category | flops | bytes accessed | tf_op | source)
XLA Modules:
  0.0 48.5 jit_solution(1666244599851512856)
XLA Ops:
  0.6 0.7 %pad_add_fusion = bf16[32,256]{1,0:T(8,128)(2,1)S(1)} fusion(bf16[32,128]{1,0:T(8,128)(2,1)} %param.15, bf16[32,128]{1,0:T(8,128)(2,1)} %param.14), kind=kLoop, calls=%fused_computation | loop fusion | flops 32768 | bytes 32768 | tf_op jit(solution)/shard_map/add | solution.py:413
  1.4 14.4 %all_to_all.17 = bf16[8,32,256]{2,1,0:T(8,128)(2,1)S(1)} all-to-all(bf16[8,32,256]{2,1,0:T(8,128)(2,1)S(1)} %broadcast_in_dim.2), channel_id=1, replica_groups={{0,2,4,6,8,10,12,14},{1,3,5,7,9,11,13,15},{16,18,20,22,24,26,28,30},{17..., dimensions={0} | all-to-all | bytes 262144 | tf_op jit(solution)/shard_map/all_to_all | solution.py:28
  15.8 0.0 copy-start
  15.8 0.0 collective-permute-start
  15.8 1.3 %collective-permute-done.other_hbm = bf16[256,256]{1,0:T(8,128)(2,1)S(1)} collective-permute-done((bf16[256,256]{1,0:T(8,128)(2,1)S(1)}, bf16[256,256]{1,0:T(8,128)(2,1)S(1)}, u32[]{:S(2)}, u32[]{:S(2)}) %collective-permute-start) | collective-permute-done | bytes 131104 | tf_op jit(solution)/shard_map/ppermute | solution.py:24
  17.1 0.0 copy-done
  17.1 0.0 copy-start.1
  17.1 0.6 %copy-done.1 = bf16[256,256]{1,0:T(8,128)(2,1)} copy-done((bf16[256,256]{1,0:T(8,128)(2,1)}, bf16[256,256]{1,0:T(8,128)(2,1)S(1)}, u32[]{:S(2)}) %copy-start.1) | copy-done | bytes 131096
  17.8 15.3 %shard_map.137 = (f32[768,1024]{1,0:T(8,128)}, f32[768,128]{1,0:T(8,128)}, f32[768,128]{1,0:T(8,128)}, f32[256,256]{1,0:T(8,128)}, f32[256,256]{1,0:T(8,128)}) custom-call(s32[2]{0:T(128)} %prompt_hbm.1, s32[2]{0:T(128)} %length_hbm.1, s32[2]{0:T(128)} %begin_hbm.1, s32[16]{0:T(128)} %holder_hbm.1, bf16[768,1024]{1,0:T(8,128)(2,1)} %q_hbm.1, ...), custom_call_target="tpu_custom_call" | custom-call | tf_op jit(solution)/shard_map/pallas_call | solution.py:346
  33.1 0.2 collective-permute-start.1
  33.3 1.6 %collective-permute-done.1 = f32[256,256]{1,0:T(8,128)S(1)} collective-permute-done((f32[256,256]{1,0:T(8,128)}, f32[256,256]{1,0:T(8,128)S(1)}, u32[]{:S(2)}, u32[]{:S(2)}) %collective-permute-start.1) | collective-permute-done | bytes 262176 | tf_op jit(solution)/shard_map/ppermute | solution.py:24
  34.9 1.0 %add.11 = f32[256,256]{1,0:T(8,128)S(1)} add(f32[256,256]{1,0:T(8,128)} %get-tuple-element.13, f32[256,256]{1,0:T(8,128)S(1)} %collective-permute-done.1) | non-fusion elementwise | flops 65536 | bytes 786432 | tf_op jit(solution)/shard_map/add | solution.py:421
  35.9 11.9 %all_to_all.18 = f32[8,32,256]{2,1,0:T(8,128)S(1)} all-to-all(f32[8,32,256]{2,1,0:T(8,128)S(1)} %bitcast.2), channel_id=1, replica_groups={{0,2,4,6,8,10,12,14},{1,3,5,7,9,11,13,15},{16,18,20,22,24,26,28,30},{17..., dimensions={0} | all-to-all | bytes 524288 | tf_op jit(solution)/shard_map/all_to_all | solution.py:28
  47.9 0.6 %fusion = (f32[32,128]{1,0:T(8,128)}, f32[32,128]{1,0:T(8,128)}) fusion(f32[32,256]{1,0:T(8,128)S(1)} %reduce_sum.9), kind=kLoop, calls=%fused_computation.1 | loop fusion | bytes 65536 | tf_op jit(solution)/shard_map/slice | solution.py:423
  (2 shorter events, 0.0 us)
Async XLA Ops:
  15.8 1.4 %copy-start = (bf16[8,32,256]{2,1,0:T(8,128)(2,1)}, bf16[8,32,256]{2,1,0:T(8,128)(2,1)S(1)}, u32[]{:S(2)}) copy-start(bf16[8,32,256]{2,1,0:T(8,128)(2,1)S(1)} %all_to_all.17) | copy-start | bytes 393220
  15.8 1.3 %collective-permute-start = (bf16[256,256]{1,0:T(8,128)(2,1)S(1)}, bf16[256,256]{1,0:T(8,128)(2,1)S(1)}, u32[]{:S(2)}, u32[]{:S(2)}) collective-permute-start(bf16[256,256]{1,0:T(8,128)(2,1)S(1)} %bitcast.3), channel_id=1, source_target_pairs={{0,1},{1,0},{2,3},{3,2},{4,5},{5,4},{6,7},{7,6},{8,9},{9,8},{10,11... | collective-permute-start | bytes 393224 | tf_op jit(solution)/shard_map/ppermute | solution.py:24
  17.1 0.6 %copy-start.1 = (bf16[256,256]{1,0:T(8,128)(2,1)}, bf16[256,256]{1,0:T(8,128)(2,1)S(1)}, u32[]{:S(2)}) copy-start(bf16[256,256]{1,0:T(8,128)(2,1)S(1)} %collective-permute-done.other_hbm) | copy-start | bytes 393220
  33.1 1.8 %collective-permute-start.1 = (f32[256,256]{1,0:T(8,128)}, f32[256,256]{1,0:T(8,128)S(1)}, u32[]{:S(2)}, u32[]{:S(2)}) collective-permute-start(f32[256,256]{1,0:T(8,128)} %get-tuple-element.14), channel_id=1, source_target_pairs={{0,1},{1,0},{2,3},{3,2},{4,5},{5,4},{6,7},{7,6},{8,9},{9,8},{10,11... | collective-permute-start | bytes 786440 | tf_op jit(solution)/shard_map/ppermute | solution.py:24
where the time goes:
time: 48.8 us; the launch traced here: 48.5 us
  blocking collectives  26.3 us (54%)
  Pallas kernels  15.3 us (31%)
  waiting for transfers between devices  2.94 us (6%)
  other arithmetic  1.73 us (4%)
  local copies, waits for them, and re-layouts  1.27 us (3%)
  between operations  0.65 us (1%)
    all_to_all x2, blocking collectives, exchange(): lax.all_to_all(x, 'seq', split_axis=0, concat_axis=0, axis_index_groups=s...  26.3 us
    pallas_call x1, Pallas kernels, slot_grads(): pl.pallas_call(grad_kernel, in_specs=[hbm] * 10, out_specs=[hbm] * 5, out...  15.3 us
    ppermute x2, waiting for transfers between devices, swap_cores(): return lax.ppermute(x, 'seq', [(i, i ^ 1) for i in range(n)])  2.94 us
    add x1, other arithmetic, body(): parts = exchange(own_term + swap_cores(other_term, n), n)  0.99 us
  transfers between devices with their start and end apart: 2, of which 2 were waited for; matrix products, arithmetic and copies ran while one was open for 0% of the time, Pallas kernels for 0%

commit v1 on v0

--- a/solution.py
+++ b/solution.py
@@ -14,6 +14,8 @@
 score_scale = 0.08838834764831845
 EXP2_SCALE = score_scale * math.log2(math.e)
 MASKED = -1e30
+
+ACROSS = (((1,), (1,)), ((), ()))
 
 
 def same_core_groups(n):
@@ -194,7 +196,8 @@
         if pair == 0:
             q_copy(s * tiles + index).wait()
             g_copy(s * tiles + index).wait()
-        q2t, g2t = turned.at[buf, 0], turned.at[buf, 1]
+        lanes = slice((u % 2) * wide, (u % 2 + 1) * wide)
+        q2t, g2t = turned.at[(u // 2) % 3, 0, :, lanes], turned.at[(u // 2) % 3, 1, :, lanes]
         q2t[...] = stacked(q_all, s, index, 2 * pair, 2).T
         g2t[...] = stacked(g_all, s, index, 2 * pair, 2).T
         tops, totals, weights = [], [], []
@@ -240,20 +243,16 @@
             yield
 
     def flush_keys(s, u):
-        index, pair = units[u]
         group, columns = (u // 2) % 2, columns_of(u)
-        q4 = stacked(q_all, s, index, 2 * (pair - 1), 4)
-        kt[0:columns, :] += jnp.dot(
-            dscore16[group, 0:columns, :], q4, preferred_element_type=jnp.float32
+        kt[:, 0:columns] += lax.dot_general(
+            turned[(u // 2) % 3, 0], dscore16[group, 0:columns, :], ACROSS, preferred_element_type=jnp.float32
         )
         yield
 
     def flush_values(s, u):
-        index, pair = units[u]
         group, columns = (u // 2) % 2, columns_of(u)
-        g4 = stacked(g_all, s, index, 2 * (pair - 1), 4)
-        vt[0:columns, :] += jnp.dot(
-            prob16[group, 0:columns, :], g4, preferred_element_type=jnp.float32
+        vt[:, 0:columns] += lax.dot_general(
+            turned[(u // 2) % 3, 1], prob16[group, 0:columns, :], ACROSS, preferred_element_type=jnp.float32
         )
         yield
 
@@ -311,16 +310,18 @@
         kt[...] = jnp.zeros_like(kt)
         vt[...] = jnp.zeros_like(vt)
         slot_units(s)
-        drk_all[slot_part(s), :] = kt[prompt_len:, :] * score_scale
-        drv_all[slot_part(s), :] = vt[prompt_len:, :]
+        drk_all[slot_part(s), :] = kt[:, prompt_len:].T * score_scale
+        drv_all[slot_part(s), :] = vt[:, prompt_len:].T
+        prompt_kt = kt[:, 0:prompt_len].T * score_scale
+        prompt_vt = vt[:, 0:prompt_len].T
         drk_copy(s).start()
         drv_copy(s).start()
         for o in range(OWNERS):
             start = block_position(place[first_block + o], me, n) * prow
             target = pl.ds(pl.multiple_of(start, prow), prow)
             block = slice(o * prow, (o + 1) * prow)
-            term_ref[target, 0:width] += kt[block, :] * score_scale
-            term_ref[target, width : 2 * width] += vt[block, :]
+            term_ref[target, 0:width] += prompt_kt[block]
+            term_ref[target, width : 2 * width] += prompt_vt[block]
 
     for copy in term_copies:
         copy.start()
@@ -374,13 +375,13 @@
             pltpu.VMEM((width, total), bf16),
             pltpu.VMEM((slot_rows, TILE), f32),
             pltpu.VMEM((TILE, TILE), f32),
-            pltpu.VMEM((2, 2, width, 2 * TILE), bf16),
+            pltpu.VMEM((3, 2, width, 4 * TILE), bf16),
             pltpu.VMEM((2, total, 2 * TILE), f32),
             pltpu.VMEM((2, total, 2 * TILE), f32),
             pltpu.VMEM((2, total, 4 * TILE), bf16),
             pltpu.VMEM((2, total, 4 * TILE), bf16),
-            pltpu.VMEM((total, width), f32),
-            pltpu.VMEM((total, width), f32),
+            pltpu.VMEM((width, total), f32),
+            pltpu.VMEM((width, total), f32),
             pltpu.SemaphoreType.DMA((4,)),
             pltpu.SemaphoreType.DMA((2,)),
             pltpu.SemaphoreType.DMA((slots * tiles,)),

time: 48.8 us -> 48.2 us (0.988)
  Pallas kernels: 15.3 us -> 14.7 us
    pallas_call x1, Pallas kernels: 15.3 us -> 14.7 us  [slot_grads(): pl.pallas_call(grad_kernel, in_specs=[hbm] * 10, out_specs=[hbm] * 5, out...]
where the time goes in v1:
time: 48.2 us; the launch traced here: 47.9 us
  blocking collectives  26.3 us (55%)
  Pallas kernels  14.7 us (30%)
  waiting for transfers between devices  2.94 us (6%)
  other arithmetic  1.73 us (4%)
  local copies, waits for them, and re-layouts  1.27 us (3%)
  between operations  0.65 us (1%)
    all_to_all x2, blocking collectives, exchange(): lax.all_to_all(x, 'seq', split_axis=0, concat_axis=0, axis_index_groups=s...  26.3 us
    pallas_call x1, Pallas kernels, slot_grads(): pl.pallas_call(grad_kernel, in_specs=[hbm] * 10, out_specs=[hbm] * 5, out...  14.7 us
    ppermute x2, waiting for transfers between devices, swap_cores(): return lax.ppermute(x, 'seq', [(i, i ^ 1) for i in range(n)])  2.94 us
    add x1, other arithmetic, body(): parts = exchange(own_term + swap_cores(other_term, n), n)  0.99 us
  transfers between devices with their start and end apart: 2, of which 2 were waited for; matrix products, arithmetic and copies ran while one was open for 0% of the time, Pallas kernels for 0%

profile of v1, /device:TPU:0, one launch (start us, length us, event | category | flops | bytes accessed | tf_op | source)
XLA Modules:
  0.0 47.9 jit_solution(4210156610670508647)
XLA Ops:
  0.6 0.7 %pad_add_fusion = bf16[32,256]{1,0:T(8,128)(2,1)S(1)} fusion(bf16[32,128]{1,0:T(8,128)(2,1)} %param.15, bf16[32,128]{1,0:T(8,128)(2,1)} %param.14), kind=kLoop, calls=%fused_computation | loop fusion | flops 32768 | bytes 32768 | tf_op jit(solution)/shard_map/add | solution.py:414
  1.4 14.4 %all_to_all.17 = bf16[8,32,256]{2,1,0:T(8,128)(2,1)S(1)} all-to-all(bf16[8,32,256]{2,1,0:T(8,128)(2,1)S(1)} %broadcast_in_dim.2), channel_id=1, replica_groups={{0,2,4,6,8,10,12,14},{1,3,5,7,9,11,13,15},{16,18,20,22,24,26,28,30},{17..., dimensions={0} | all-to-all | bytes 262144 | tf_op jit(solution)/shard_map/all_to_all | solution.py:30
  15.8 0.0 copy-start
  15.8 0.0 collective-permute-start
  15.8 1.3 %collective-permute-done.other_hbm = bf16[256,256]{1,0:T(8,128)(2,1)S(1)} collective-permute-done((bf16[256,256]{1,0:T(8,128)(2,1)S(1)}, bf16[256,256]{1,0:T(8,128)(2,1)S(1)}, u32[]{:S(2)}, u32[]{:S(2)}) %collective-permute-start) | collective-permute-done | bytes 131104 | tf_op jit(solution)/shard_map/ppermute | solution.py:26
  17.1 0.0 copy-done
  17.1 0.0 copy-start.1
  17.1 0.6 %copy-done.1 = bf16[256,256]{1,0:T(8,128)(2,1)} copy-done((bf16[256,256]{1,0:T(8,128)(2,1)}, bf16[256,256]{1,0:T(8,128)(2,1)S(1)}, u32[]{:S(2)}) %copy-start.1) | copy-done | bytes 131096
  17.8 14.7 %shard_map.137 = (f32[768,1024]{1,0:T(8,128)}, f32[768,128]{1,0:T(8,128)}, f32[768,128]{1,0:T(8,128)}, f32[256,256]{1,0:T(8,128)}, f32[256,256]{1,0:T(8,128)}) custom-call(s32[2]{0:T(128)} %prompt_hbm.1, s32[2]{0:T(128)} %length_hbm.1, s32[2]{0:T(128)} %begin_hbm.1, s32[16]{0:T(128)} %holder_hbm.1, bf16[768,1024]{1,0:T(8,128)(2,1)} %q_hbm.1, ...), custom_call_target="tpu_custom_call" | custom-call | tf_op jit(solution)/shard_map/pallas_call | solution.py:347
  32.5 0.2 collective-permute-start.1
  32.7 1.6 %collective-permute-done.1 = f32[256,256]{1,0:T(8,128)S(1)} collective-permute-done((f32[256,256]{1,0:T(8,128)}, f32[256,256]{1,0:T(8,128)S(1)}, u32[]{:S(2)}, u32[]{:S(2)}) %collective-permute-start.1) | collective-permute-done | bytes 262176 | tf_op jit(solution)/shard_map/ppermute | solution.py:26
  34.3 1.0 %add.11 = f32[256,256]{1,0:T(8,128)S(1)} add(f32[256,256]{1,0:T(8,128)} %get-tuple-element.13, f32[256,256]{1,0:T(8,128)S(1)} %collective-permute-done.1) | non-fusion elementwise | flops 65536 | bytes 786432 | tf_op jit(solution)/shard_map/add | solution.py:422
  35.3 11.9 %all_to_all.18 = f32[8,32,256]{2,1,0:T(8,128)S(1)} all-to-all(f32[8,32,256]{2,1,0:T(8,128)S(1)} %bitcast.2), channel_id=1, replica_groups={{0,2,4,6,8,10,12,14},{1,3,5,7,9,11,13,15},{16,18,20,22,24,26,28,30},{17..., dimensions={0} | all-to-all | bytes 524288 | tf_op jit(solution)/shard_map/all_to_all | solution.py:30
  47.3 0.6 %fusion = (f32[32,128]{1,0:T(8,128)}, f32[32,128]{1,0:T(8,128)}) fusion(f32[32,256]{1,0:T(8,128)S(1)} %reduce_sum.9), kind=kLoop, calls=%fused_computation.1 | loop fusion | bytes 65536 | tf_op jit(solution)/shard_map/slice | solution.py:424
  (2 shorter events, 0.0 us)
Async XLA Ops:
  15.8 1.4 %copy-start = (bf16[8,32,256]{2,1,0:T(8,128)(2,1)}, bf16[8,32,256]{2,1,0:T(8,128)(2,1)S(1)}, u32[]{:S(2)}) copy-start(bf16[8,32,256]{2,1,0:T(8,128)(2,1)S(1)} %all_to_all.17) | copy-start | bytes 393220
  15.8 1.3 %collective-permute-start = (bf16[256,256]{1,0:T(8,128)(2,1)S(1)}, bf16[256,256]{1,0:T(8,128)(2,1)S(1)}, u32[]{:S(2)}, u32[]{:S(2)}) collective-permute-start(bf16[256,256]{1,0:T(8,128)(2,1)S(1)} %bitcast.3), channel_id=1, source_target_pairs={{0,1},{1,0},{2,3},{3,2},{4,5},{5,4},{6,7},{7,6},{8,9},{9,8},{10,11... | collective-permute-start | bytes 393224 | tf_op jit(solution)/shard_map/ppermute | solution.py:26
  17.1 0.6 %copy-start.1 = (bf16[256,256]{1,0:T(8,128)(2,1)}, bf16[256,256]{1,0:T(8,128)(2,1)S(1)}, u32[]{:S(2)}) copy-start(bf16[256,256]{1,0:T(8,128)(2,1)S(1)} %collective-permute-done.other_hbm) | copy-start | bytes 393220
  32.5 1.8 %collective-permute-start.1 = (f32[256,256]{1,0:T(8,128)}, f32[256,256]{1,0:T(8,128)S(1)}, u32[]{:S(2)}, u32[]{:S(2)}) collective-permute-start(f32[256,256]{1,0:T(8,128)} %get-tuple-element.14), channel_id=1, source_target_pairs={{0,1},{1,0},{2,3},{3,2},{4,5},{5,4},{6,7},{7,6},{8,9},{9,8},{10,11... | collective-permute-start | bytes 786440 | tf_op jit(solution)/shard_map/ppermute | solution.py:26

commit v2 on v1

--- a/solution.py
+++ b/solution.py
@@ -171,50 +171,94 @@
     def _(j):
         place[holder_ref[j]] = j
 
-    half = heads // 2
     wide = 2 * TILE
-    units = [(index, pair) for index in range(tiles) for pair in range(half)]
+    at_once = 4
+    groups = heads // at_once
+    units = [(s, index, g) for s in range(slots) for index in range(tiles) for g in range(groups)]
 
     def columns_of(u):
-        return prompt_len + (units[u][0] + 1) * TILE
+        return prompt_len + (units[u][1] + 1) * TILE
+
+    def rows_of(u):
+        s, index, _ = units[u]
+        first = (s * tiles + index) * TILE
+        return slice(first, first + TILE)
+
+    def first_head(u, side):
+        return units[u][2] * at_once + 2 * side
 
     def chunks(u):
         return range(0, columns_of(u), TILE)
 
-    def stacked(ref, s, index, first, count):
-        part = tile_rows(s * tiles + index)
+    def lanes_of(side):
+        return slice(side * wide, (side + 1) * wide)
+
+    def stacked(ref, u, side):
+        first = first_head(u, side)
         return jnp.concatenate(
-            [ref[part, (first + h) * width : (first + h + 1) * width] for h in range(count)], axis=0
+            [ref[rows_of(u), (first + h) * width : (first + h + 1) * width] for h in range(2)], axis=0
         )
 
     def fold(x, how):
         return how(how(x.reshape(x.shape[0] // 8, 8, x.shape[1]), axis=0), axis=0, keepdims=True)
 
-    def head(s, u, out):
-        index, pair = units[u]
+    def prepare(s):
+        first_block = prompt_ref[s] * OWNERS
+        for o in range(OWNERS):
+            start = block_position(place[first_block + o], me, n) * prow
+            source = pl.ds(pl.multiple_of(start, prow), prow)
+            keys[s, o * prow : (o + 1) * prow, :] = kv[source, 0:width]
+            values[s, o * prow : (o + 1) * prow, :] = kv[source, width : 2 * width]
+        own = slice(s * slot_rows, (s + 1) * slot_rows)
+        keys[s, prompt_len:, :] = rk_all[own, :]
+        values[s, prompt_len:, :] = rv_all[own, :]
+        yield
+        keys_t[s] = keys[s].astype(jnp.float32).T.astype(jnp.bfloat16)
+        yield
+        column = lax.broadcasted_iota(jnp.int32, (slot_rows, TILE), 0)
+        live_bias[s] = jnp.where(column >= begin_ref[s], 0.0, MASKED)
+        kt[s] = jnp.zeros_like(kt[s])
+        vt[s] = jnp.zeros_like(vt[s])
+        yield
+
+    def finish(s):
+        own = slice(s * slot_rows, (s + 1) * slot_rows)
+        prompt_kt = kt[s, :, 0:prompt_len].T * score_scale
+        prompt_vt = vt[s, :, 0:prompt_len].T
+        yield
+        drk_all[own, :] = kt[s, :, prompt_len:].T * score_scale
+        drv_all[own, :] = vt[s, :, prompt_len:].T
+        yield
+        first_block = prompt_ref[s] * OWNERS
+        for o in range(OWNERS):
+            start = block_position(place[first_block + o], me, n) * prow
+            target = pl.ds(pl.multiple_of(start, prow), prow)
+            block = slice(o * prow, (o + 1) * prow)
+            term_ref[target, 0:width] += prompt_kt[block]
+            term_ref[target, width : 2 * width] += prompt_vt[block]
+        yield
+
+    def head(u, side, out):
+        s, index, _ = units[u]
         columns, buf = columns_of(u), u % 2
-        if pair == 0:
-            q_copy(s * tiles + index).wait()
-            g_copy(s * tiles + index).wait()
-        lanes = slice((u % 2) * wide, (u % 2 + 1) * wide)
-        q2t, g2t = turned.at[(u // 2) % 3, 0, :, lanes], turned.at[(u // 2) % 3, 1, :, lanes]
-        q2t[...] = stacked(q_all, s, index, 2 * pair, 2).T
-        g2t[...] = stacked(g_all, s, index, 2 * pair, 2).T
+        q2t, g2t = turned.at[u % 3, 0, :, lanes_of(side)], turned.at[u % 3, 1, :, lanes_of(side)]
+        q2t[...] = stacked(q_all, u, side).T
+        g2t[...] = stacked(g_all, u, side).T
         tops, totals, weights = [], [], []
         for c in chunks(u):
             part = slice(c, c + TILE)
-            block = jnp.dot(keys[part, :], q2t[...], preferred_element_type=jnp.float32)
+            block = jnp.dot(keys[s, part, :], q2t[...], preferred_element_type=jnp.float32)
             if c >= prompt_len:
-                bias = live_bias[c - prompt_len : c - prompt_len + TILE, :]
+                bias = live_bias[s, c - prompt_len : c - prompt_len + TILE, :]
                 if c + TILE == columns:
                     bias = bias + causal_bias[...]
                 block = block + jnp.concatenate([bias, bias], axis=1)
             top = fold(block, jnp.max) * EXP2_SCALE
             e = jnp.exp2(block * EXP2_SCALE - top)
-            exps[buf, part, :] = e
+            exps[buf, side, part, :] = e
             yield
-            d = jnp.dot(values[part, :], g2t[...], preferred_element_type=jnp.float32)
-            dprobs[buf, part, :] = d
+            d = jnp.dot(values[s, part, :], g2t[...], preferred_element_type=jnp.float32)
+            dprobs[buf, side, part, :] = d
             tops.append(top)
             totals.append(fold(e, jnp.sum))
             weights.append(fold(e * d, jnp.sum))
@@ -229,46 +273,42 @@
         out["delta"] = weighted * inverse
         out["factors"] = [f * inverse for f in factors]
 
-    def tail(u, stats):
-        buf, group = u % 2, (u // 2) % 2
-        lanes = slice((u % 2) * wide, (u % 2 + 1) * wide)
+    def tail(u, side, stats):
+        buf, lanes = u % 2, lanes_of(side)
         delta = stats["delta"]
         for c, factor in zip(chunks(u), stats["factors"]):
             for first in range(c, c + TILE, PIECE):
                 part = slice(first, first + PIECE)
-                p = exps[buf, part, :] * factor
-                prob16[group, part, lanes] = p.astype(jnp.bfloat16)
-                ds = p * (dprobs[buf, part, :] - delta)
-                dscore16[group, part, lanes] = ds.astype(jnp.bfloat16)
+                p = exps[buf, side, part, :] * factor
+                prob16[buf, part, lanes] = p.astype(jnp.bfloat16)
+                ds = p * (dprobs[buf, side, part, :] - delta)
+                dscore16[buf, part, lanes] = ds.astype(jnp.bfloat16)
             yield
 
-    def flush_keys(s, u):
-        group, columns = (u // 2) % 2, columns_of(u)
-        kt[:, 0:columns] += lax.dot_general(
-            turned[(u // 2) % 3, 0], dscore16[group, 0:columns, :], ACROSS, preferred_element_type=jnp.float32
-        )
-        yield
-
-    def flush_values(s, u):
-        group, columns = (u // 2) % 2, columns_of(u)
-        vt[:, 0:columns] += lax.dot_general(
-            turned[(u // 2) % 3, 1], prob16[group, 0:columns, :], ACROSS, preferred_element_type=jnp.float32
-        )
-        yield
-
-    def flush_queries(s, u):
-        index, pair = units[u]
-        group, columns = (u // 2) % 2, columns_of(u)
-        part = tile_rows(s * tiles + index)
+    def flush_keys(u):
+        s, columns = units[u][0], columns_of(u)
+        kt[s, :, 0:columns] += lax.dot_general(
+            turned[u % 3, 0], dscore16[u % 2, 0:columns, :], ACROSS, preferred_element_type=jnp.float32
+        )
+        yield
+
+    def flush_values(u):
+        s, columns = units[u][0], columns_of(u)
+        vt[s, :, 0:columns] += lax.dot_general(
+            turned[u % 3, 1], prob16[u % 2, 0:columns, :], ACROSS, preferred_element_type=jnp.float32
+        )
+        yield
+
+    def flush_queries(u):
+        s, columns = units[u][0], columns_of(u)
         for side in range(2):
-            ds = dscore16[group, 0:columns, side * wide : (side + 1) * wide]
-            dqt = jnp.dot(keys_t[:, 0:columns], ds, preferred_element_type=jnp.float32)
+            ds = dscore16[u % 2, 0:columns, lanes_of(side)]
+            dqt = jnp.dot(keys_t[s, :, 0:columns], ds, preferred_element_type=jnp.float32)
             for h in range(2):
-                first = (2 * (pair - 1 + side) + h) * width
-                dq_all[part, first : first + width] = dqt[:, h * TILE : (h + 1) * TILE].T * score_scale
+                first = (first_head(u, side) + h) * width
+                dq = dqt[:, h * TILE : (h + 1) * TILE].T * score_scale
+                dq_all[rows_of(u), first : first + width] = dq
             yield
-        if pair == half - 1:
-            dq_copy(s * tiles + index).start()
 
     def together(*steps):
         steps = list(steps)
@@ -277,51 +317,46 @@
                 if next(step, steps) is steps:
                     steps.remove(step)
 
-    def slot_units(s):
-        stats = {}
-        together(head(s, 0, stats))
-        for u in range(len(units)):
-            now, stats = stats, {}
-            steps = []
-            if u + 1 < len(units):
-                steps.append(head(s, u + 1, stats))
-            steps.append(tail(u, now))
-            if u >= 2 and u % 2 == 0:
-                steps += [flush_keys(s, u - 1), flush_queries(s, u - 1)]
-            elif u >= 2:
-                steps.append(flush_values(s, u - 2))
-            together(*steps)
-        last = len(units) - 1
-        together(flush_keys(s, last), flush_values(s, last), flush_queries(s, last))
-
-    @pl.loop(0, slots)
-    def _(s):
-        first_block = prompt_ref[s] * OWNERS
-        for o in range(OWNERS):
-            start = block_position(place[first_block + o], me, n) * prow
-            source = pl.ds(pl.multiple_of(start, prow), prow)
-            keys[o * prow : (o + 1) * prow, :] = kv[source, 0:width]
-            values[o * prow : (o + 1) * prow, :] = kv[source, width : 2 * width]
-        keys[prompt_len:, :] = rk_all[slot_part(s), :]
-        values[prompt_len:, :] = rv_all[slot_part(s), :]
-        keys_t[...] = keys[...].astype(jnp.float32).T.astype(jnp.bfloat16)
-        column = lax.broadcasted_iota(jnp.int32, (slot_rows, TILE), 0)
-        live_bias[...] = jnp.where(column >= begin_ref[s], 0.0, MASKED)
-        kt[...] = jnp.zeros_like(kt)
-        vt[...] = jnp.zeros_like(vt)
-        slot_units(s)
-        drk_all[slot_part(s), :] = kt[:, prompt_len:].T * score_scale
-        drv_all[slot_part(s), :] = vt[:, prompt_len:].T
-        prompt_kt = kt[:, 0:prompt_len].T * score_scale
-        prompt_vt = vt[:, 0:prompt_len].T
-        drk_copy(s).start()
-        drv_copy(s).start()
-        for o in range(OWNERS):
-            start = block_position(place[first_block + o], me, n) * prow
-            target = pl.ds(pl.multiple_of(start, prow), prow)
-            block = slice(o * prow, (o + 1) * prow)
-            term_ref[target, 0:width] += prompt_kt[block]
-            term_ref[target, width : 2 * width] += prompt_vt[block]
+    def wait_rows(u):
+        s, index, g = units[u]
+        if g == 0:
+            q_copy(s * tiles + index).wait()
+            g_copy(s * tiles + index).wait()
+
+    count = len(units)
+    per_slot = tiles * groups
+    stats = [({}, {}) for _ in units]
+    together(prepare(0))
+    wait_rows(0)
+    together(head(0, 0, stats[0][0]))
+    for u in range(count):
+        s = units[u][0]
+        steps = [head(u, 1, stats[u][1]), tail(u, 0, stats[u][0])]
+        if u >= 1:
+            steps += [flush_keys(u - 1), flush_queries(u - 1)]
+        if u % per_slot == 2 and s + 1 < slots:
+            steps.append(prepare(s + 1))
+        if u % per_slot == 1 and s >= 1:
+            steps.append(finish(s - 1))
+        together(*steps)
+        if u >= 1 and units[u - 1][2] == groups - 1:
+            dq_copy(units[u - 1][0] * tiles + units[u - 1][1]).start()
+        if u % per_slot == 1 and s >= 1:
+            drk_copy(s - 1).start()
+            drv_copy(s - 1).start()
+        steps = []
+        if u + 1 < count:
+            wait_rows(u + 1)
+            steps.append(head(u + 1, 0, stats[u + 1][0]))
+        steps.append(tail(u, 1, stats[u][1]))
+        if u >= 1:
+            steps.append(flush_values(u - 1))
+        together(*steps)
+    together(flush_keys(count - 1), flush_values(count - 1), flush_queries(count - 1))
+    dq_copy(slots * tiles - 1).start()
+    together(finish(slots - 1))
+    drk_copy(slots - 1).start()
+    drv_copy(slots - 1).start()
 
     for copy in term_copies:
         copy.start()
@@ -370,18 +405,18 @@
             pltpu.VMEM((rows, width), f32),
             pltpu.VMEM((n * prow, 2 * width), bf16),
             pltpu.VMEM((n * prow, 2 * width), f32),
-            pltpu.VMEM((total, width), bf16),
-            pltpu.VMEM((total, width), bf16),
-            pltpu.VMEM((width, total), bf16),
-            pltpu.VMEM((slot_rows, TILE), f32),
+            pltpu.VMEM((slots, total, width), bf16),
+            pltpu.VMEM((slots, total, width), bf16),
+            pltpu.VMEM((slots, width, total), bf16),
+            pltpu.VMEM((slots, slot_rows, TILE), f32),
             pltpu.VMEM((TILE, TILE), f32),
             pltpu.VMEM((3, 2, width, 4 * TILE), bf16),
-            pltpu.VMEM((2, total, 2 * TILE), f32),
-            pltpu.VMEM((2, total, 2 * TILE), f32),
+            pltpu.VMEM((2, 2, total, 2 * TILE), f32),
+            pltpu.VMEM((2, 2, total, 2 * TILE), f32),
             pltpu.VMEM((2, total, 4 * TILE), bf16),
             pltpu.VMEM((2, total, 4 * TILE), bf16),
-            pltpu.VMEM((width, total), f32),
-            pltpu.VMEM((width, total), f32),
+            pltpu.VMEM((slots, width, total), f32),
+            pltpu.VMEM((slots, width, total), f32),
             pltpu.SemaphoreType.DMA((4,)),
             pltpu.SemaphoreType.DMA((2,)),
             pltpu.SemaphoreType.DMA((slots * tiles,)),

time: 48.2 us -> 48 us (level)
  no operation moved by 1% of the time
where the time goes in v2:
time: 48 us; the launch traced here: 47.7 us
  blocking collectives  26.3 us (55%)
  Pallas kernels  14.5 us (30%)
  waiting for transfers between devices  2.94 us (6%)
  other arithmetic  1.73 us (4%)
  local copies, waits for them, and re-layouts  1.27 us (3%)
  between operations  0.65 us (1%)
    all_to_all x2, blocking collectives, exchange(): lax.all_to_all(x, 'seq', split_axis=0, concat_axis=0, axis_index_groups=s...  26.3 us
    pallas_call x1, Pallas kernels, slot_grads(): pl.pallas_call(grad_kernel, in_specs=[hbm] * 10, out_specs=[hbm] * 5, out...  14.5 us
    ppermute x2, waiting for transfers between devices, swap_cores(): return lax.ppermute(x, 'seq', [(i, i ^ 1) for i in range(n)])  2.94 us
    add x1, other arithmetic, body(): parts = exchange(own_term + swap_cores(other_term, n), n)  0.99 us
  transfers between devices with their start and end apart: 2, of which 2 were waited for; matrix products, arithmetic and copies ran while one was open for 0% of the time, Pallas kernels for 0%

profile of v2, /device:TPU:0, one launch (start us, length us, event | category | flops | bytes accessed | tf_op | source)
XLA Modules:
  0.0 47.7 jit_solution(7276249600649213485)
XLA Ops:
  0.6 0.7 %pad_add_fusion = bf16[32,256]{1,0:T(8,128)(2,1)S(1)} fusion(bf16[32,128]{1,0:T(8,128)(2,1)} %param.15, bf16[32,128]{1,0:T(8,128)(2,1)} %param.14), kind=kLoop, calls=%fused_computation | loop fusion | flops 32768 | bytes 32768 | tf_op jit(solution)/shard_map/add | solution.py:449
  1.4 14.4 %all_to_all.17 = bf16[8,32,256]{2,1,0:T(8,128)(2,1)S(1)} all-to-all(bf16[8,32,256]{2,1,0:T(8,128)(2,1)S(1)} %broadcast_in_dim.2), channel_id=1, replica_groups={{0,2,4,6,8,10,12,14},{1,3,5,7,9,11,13,15},{16,18,20,22,24,26,28,30},{17..., dimensions={0} | all-to-all | bytes 262144 | tf_op jit(solution)/shard_map/all_to_all | solution.py:30
  15.8 0.0 copy-start
  15.8 0.0 collective-permute-start
  15.8 1.3 %collective-permute-done.other_hbm = bf16[256,256]{1,0:T(8,128)(2,1)S(1)} collective-permute-done((bf16[256,256]{1,0:T(8,128)(2,1)S(1)}, bf16[256,256]{1,0:T(8,128)(2,1)S(1)}, u32[]{:S(2)}, u32[]{:S(2)}) %collective-permute-start) | collective-permute-done | bytes 131104 | tf_op jit(solution)/shard_map/ppermute | solution.py:26
  17.1 0.0 copy-done
  17.1 0.0 copy-start.1
  17.1 0.6 %copy-done.1 = bf16[256,256]{1,0:T(8,128)(2,1)} copy-done((bf16[256,256]{1,0:T(8,128)(2,1)}, bf16[256,256]{1,0:T(8,128)(2,1)S(1)}, u32[]{:S(2)}) %copy-start.1) | copy-done | bytes 131096
  17.8 14.5 %shard_map.137 = (f32[768,1024]{1,0:T(8,128)}, f32[768,128]{1,0:T(8,128)}, f32[768,128]{1,0:T(8,128)}, f32[256,256]{1,0:T(8,128)}, f32[256,256]{1,0:T(8,128)}) custom-call(s32[2]{0:T(128)} %prompt_hbm.1, s32[2]{0:T(128)} %length_hbm.1, s32[2]{0:T(128)} %begin_hbm.1, s32[16]{0:T(128)} %holder_hbm.1, bf16[768,1024]{1,0:T(8,128)(2,1)} %q_hbm.1, ...), custom_call_target="tpu_custom_call" | custom-call | tf_op jit(solution)/shard_map/pallas_call | solution.py:382
  32.3 0.2 collective-permute-start.1
  32.5 1.6 %collective-permute-done.1 = f32[256,256]{1,0:T(8,128)S(1)} collective-permute-done((f32[256,256]{1,0:T(8,128)}, f32[256,256]{1,0:T(8,128)S(1)}, u32[]{:S(2)}, u32[]{:S(2)}) %collective-permute-start.1) | collective-permute-done | bytes 262176 | tf_op jit(solution)/shard_map/ppermute | solution.py:26
  34.1 1.0 %add.11 = f32[256,256]{1,0:T(8,128)S(1)} add(f32[256,256]{1,0:T(8,128)} %get-tuple-element.13, f32[256,256]{1,0:T(8,128)S(1)} %collective-permute-done.1) | non-fusion elementwise | flops 65536 | bytes 786432 | tf_op jit(solution)/shard_map/add | solution.py:457
  35.1 11.9 %all_to_all.18 = f32[8,32,256]{2,1,0:T(8,128)S(1)} all-to-all(f32[8,32,256]{2,1,0:T(8,128)S(1)} %bitcast.2), channel_id=1, replica_groups={{0,2,4,6,8,10,12,14},{1,3,5,7,9,11,13,15},{16,18,20,22,24,26,28,30},{17..., dimensions={0} | all-to-all | bytes 524288 | tf_op jit(solution)/shard_map/all_to_all | solution.py:30
  47.1 0.6 %fusion = (f32[32,128]{1,0:T(8,128)}, f32[32,128]{1,0:T(8,128)}) fusion(f32[32,256]{1,0:T(8,128)S(1)} %reduce_sum.9), kind=kLoop, calls=%fused_computation.1 | loop fusion | bytes 65536 | tf_op jit(solution)/shard_map/slice | solution.py:459
  (2 shorter events, 0.0 us)
Async XLA Ops:
  15.8 1.4 %copy-start = (bf16[8,32,256]{2,1,0:T(8,128)(2,1)}, bf16[8,32,256]{2,1,0:T(8,128)(2,1)S(1)}, u32[]{:S(2)}) copy-start(bf16[8,32,256]{2,1,0:T(8,128)(2,1)S(1)} %all_to_all.17) | copy-start | bytes 393220
  15.8 1.3 %collective-permute-start = (bf16[256,256]{1,0:T(8,128)(2,1)S(1)}, bf16[256,256]{1,0:T(8,128)(2,1)S(1)}, u32[]{:S(2)}, u32[]{:S(2)}) collective-permute-start(bf16[256,256]{1,0:T(8,128)(2,1)S(1)} %bitcast.3), channel_id=1, source_target_pairs={{0,1},{1,0},{2,3},{3,2},{4,5},{5,4},{6,7},{7,6},{8,9},{9,8},{10,11... | collective-permute-start | bytes 393224 | tf_op jit(solution)/shard_map/ppermute | solution.py:26
  17.1 0.6 %copy-start.1 = (bf16[256,256]{1,0:T(8,128)(2,1)}, bf16[256,256]{1,0:T(8,128)(2,1)S(1)}, u32[]{:S(2)}) copy-start(bf16[256,256]{1,0:T(8,128)(2,1)S(1)} %collective-permute-done.other_hbm) | copy-start | bytes 393220
  32.3 1.8 %collective-permute-start.1 = (f32[256,256]{1,0:T(8,128)}, f32[256,256]{1,0:T(8,128)S(1)}, u32[]{:S(2)}, u32[]{:S(2)}) collective-permute-start(f32[256,256]{1,0:T(8,128)} %get-tuple-element.14), channel_id=1, source_target_pairs={{0,1},{1,0},{2,3},{3,2},{4,5},{5,4},{6,7},{7,6},{8,9},{9,8},{10,11... | collective-permute-start | bytes 786440 | tf_op jit(solution)/shard_map/ppermute | solution.py:26

commit v3 on v2

--- a/solution.py
+++ b/solution.py
@@ -245,9 +245,11 @@
         q2t[...] = stacked(q_all, u, side).T
         g2t[...] = stacked(g_all, u, side).T
         tops, totals, weights = [], [], []
+        all_scores = jnp.dot(keys[s, 0:columns, :], q2t[...], preferred_element_type=jnp.float32)
+        all_dprobs = jnp.dot(values[s, 0:columns, :], g2t[...], preferred_element_type=jnp.float32)
         for c in chunks(u):
             part = slice(c, c + TILE)
-            block = jnp.dot(keys[s, part, :], q2t[...], preferred_element_type=jnp.float32)
+            block = all_scores[part]
             if c >= prompt_len:
                 bias = live_bias[s, c - prompt_len : c - prompt_len + TILE, :]
                 if c + TILE == columns:
@@ -257,7 +259,7 @@
             e = jnp.exp2(block * EXP2_SCALE - top)
             exps[buf, side, part, :] = e
             yield
-            d = jnp.dot(values[s, part, :], g2t[...], preferred_element_type=jnp.float32)
+            d = all_dprobs[part]
             dprobs[buf, side, part, :] = d
             tops.append(top)
             totals.append(fold(e, jnp.sum))

time: 48 us -> 48.1 us (level)
  no operation moved by 1% of the time
where the time goes in v3:
time: 48.1 us; the launch traced here: 47.8 us
  blocking collectives  26.3 us (55%)
  Pallas kernels  14.6 us (30%)
  waiting for transfers between devices  2.94 us (6%)
  other arithmetic  1.73 us (4%)
  local copies, waits for them, and re-layouts  1.27 us (3%)
  between operations  0.65 us (1%)
    all_to_all x2, blocking collectives, exchange(): lax.all_to_all(x, 'seq', split_axis=0, concat_axis=0, axis_index_groups=s...  26.3 us
    pallas_call x1, Pallas kernels, slot_grads(): pl.pallas_call(grad_kernel, in_specs=[hbm] * 10, out_specs=[hbm] * 5, out...  14.6 us
    ppermute x2, waiting for transfers between devices, swap_cores(): return lax.ppermute(x, 'seq', [(i, i ^ 1) for i in range(n)])  2.94 us
    add x1, other arithmetic, body(): parts = exchange(own_term + swap_cores(other_term, n), n)  0.99 us
  transfers between devices with their start and end apart: 2, of which 2 were waited for; matrix products, arithmetic and copies ran while one was open for 0% of the time, Pallas kernels for 0%

profile of v3, /device:TPU:0, one launch (start us, length us, event | category | flops | bytes accessed | tf_op | source)
XLA Modules:
  0.0 47.8 jit_solution(184820088172518646)
XLA Ops:
  0.6 0.7 %pad_add_fusion = bf16[32,256]{1,0:T(8,128)(2,1)S(1)} fusion(bf16[32,128]{1,0:T(8,128)(2,1)} %param.15, bf16[32,128]{1,0:T(8,128)(2,1)} %param.14), kind=kLoop, calls=%fused_computation | loop fusion | flops 32768 | bytes 32768 | tf_op jit(solution)/shard_map/add | solution.py:451
  1.4 14.4 %all_to_all.17 = bf16[8,32,256]{2,1,0:T(8,128)(2,1)S(1)} all-to-all(bf16[8,32,256]{2,1,0:T(8,128)(2,1)S(1)} %broadcast_in_dim.2), channel_id=1, replica_groups={{0,2,4,6,8,10,12,14},{1,3,5,7,9,11,13,15},{16,18,20,22,24,26,28,30},{17..., dimensions={0} | all-to-all | bytes 262144 | tf_op jit(solution)/shard_map/all_to_all | solution.py:30
  15.8 0.0 copy-start
  15.8 0.0 collective-permute-start
  15.8 1.3 %collective-permute-done.other_hbm = bf16[256,256]{1,0:T(8,128)(2,1)S(1)} collective-permute-done((bf16[256,256]{1,0:T(8,128)(2,1)S(1)}, bf16[256,256]{1,0:T(8,128)(2,1)S(1)}, u32[]{:S(2)}, u32[]{:S(2)}) %collective-permute-start) | collective-permute-done | bytes 131104 | tf_op jit(solution)/shard_map/ppermute | solution.py:26
  17.1 0.0 copy-done
  17.1 0.0 copy-start.1
  17.1 0.6 %copy-done.1 = bf16[256,256]{1,0:T(8,128)(2,1)} copy-done((bf16[256,256]{1,0:T(8,128)(2,1)}, bf16[256,256]{1,0:T(8,128)(2,1)S(1)}, u32[]{:S(2)}) %copy-start.1) | copy-done | bytes 131096
  17.8 14.6 %shard_map.137 = (f32[768,1024]{1,0:T(8,128)}, f32[768,128]{1,0:T(8,128)}, f32[768,128]{1,0:T(8,128)}, f32[256,256]{1,0:T(8,128)}, f32[256,256]{1,0:T(8,128)}) custom-call(s32[2]{0:T(128)} %prompt_hbm.1, s32[2]{0:T(128)} %length_hbm.1, s32[2]{0:T(128)} %begin_hbm.1, s32[16]{0:T(128)} %holder_hbm.1, bf16[768,1024]{1,0:T(8,128)(2,1)} %q_hbm.1, ...), custom_call_target="tpu_custom_call" | custom-call | tf_op jit(solution)/shard_map/pallas_call | solution.py:384
  32.4 0.2 collective-permute-start.1
  32.6 1.6 %collective-permute-done.1 = f32[256,256]{1,0:T(8,128)S(1)} collective-permute-done((f32[256,256]{1,0:T(8,128)}, f32[256,256]{1,0:T(8,128)S(1)}, u32[]{:S(2)}, u32[]{:S(2)}) %collective-permute-start.1) | collective-permute-done | bytes 262176 | tf_op jit(solution)/shard_map/ppermute | solution.py:26
  34.2 1.0 %add.11 = f32[256,256]{1,0:T(8,128)S(1)} add(f32[256,256]{1,0:T(8,128)} %get-tuple-element.13, f32[256,256]{1,0:T(8,128)S(1)} %collective-permute-done.1) | non-fusion elementwise | flops 65536 | bytes 786432 | tf_op jit(solution)/shard_map/add | solution.py:459
  35.2 11.9 %all_to_all.18 = f32[8,32,256]{2,1,0:T(8,128)S(1)} all-to-all(f32[8,32,256]{2,1,0:T(8,128)S(1)} %bitcast.2), channel_id=1, replica_groups={{0,2,4,6,8,10,12,14},{1,3,5,7,9,11,13,15},{16,18,20,22,24,26,28,30},{17..., dimensions={0} | all-to-all | bytes 524288 | tf_op jit(solution)/shard_map/all_to_all | solution.py:30
  47.2 0.6 %fusion = (f32[32,128]{1,0:T(8,128)}, f32[32,128]{1,0:T(8,128)}) fusion(f32[32,256]{1,0:T(8,128)S(1)} %reduce_sum.9), kind=kLoop, calls=%fused_computation.1 | loop fusion | bytes 65536 | tf_op jit(solution)/shard_map/slice | solution.py:461
  (2 shorter events, 0.0 us)
Async XLA Ops:
  15.8 1.4 %copy-start = (bf16[8,32,256]{2,1,0:T(8,128)(2,1)}, bf16[8,32,256]{2,1,0:T(8,128)(2,1)S(1)}, u32[]{:S(2)}) copy-start(bf16[8,32,256]{2,1,0:T(8,128)(2,1)S(1)} %all_to_all.17) | copy-start | bytes 393220
  15.8 1.3 %collective-permute-start = (bf16[256,256]{1,0:T(8,128)(2,1)S(1)}, bf16[256,256]{1,0:T(8,128)(2,1)S(1)}, u32[]{:S(2)}, u32[]{:S(2)}) collective-permute-start(bf16[256,256]{1,0:T(8,128)(2,1)S(1)} %bitcast.3), channel_id=1, source_target_pairs={{0,1},{1,0},{2,3},{3,2},{4,5},{5,4},{6,7},{7,6},{8,9},{9,8},{10,11... | collective-permute-start | bytes 393224 | tf_op jit(solution)/shard_map/ppermute | solution.py:26
  17.1 0.6 %copy-start.1 = (bf16[256,256]{1,0:T(8,128)(2,1)}, bf16[256,256]{1,0:T(8,128)(2,1)S(1)}, u32[]{:S(2)}) copy-start(bf16[256,256]{1,0:T(8,128)(2,1)S(1)} %collective-permute-done.other_hbm) | copy-start | bytes 393220
  32.4 1.8 %collective-permute-start.1 = (f32[256,256]{1,0:T(8,128)}, f32[256,256]{1,0:T(8,128)S(1)}, u32[]{:S(2)}, u32[]{:S(2)}) collective-permute-start(f32[256,256]{1,0:T(8,128)} %get-tuple-element.14), channel_id=1, source_target_pairs={{0,1},{1,0},{2,3},{3,2},{4,5},{5,4},{6,7},{7,6},{8,9},{9,8},{10,11... | collective-permute-start | bytes 786440 | tf_op jit(solution)/shard_map/ppermute | solution.py:26

commit v4 on v2

--- a/solution.py
+++ b/solution.py
@@ -283,39 +283,44 @@
                 prob16[buf, part, lanes] = p.astype(jnp.bfloat16)
                 ds = p * (dprobs[buf, side, part, :] - delta)
                 dscore16[buf, part, lanes] = ds.astype(jnp.bfloat16)
+                yield
+
+    def flush_keys(u):
+        s = units[u][0]
+        for c in chunks(u):
+            part = slice(c, c + TILE)
+            kt[s, :, part] += lax.dot_general(
+                turned[u % 3, 0], dscore16[u % 2, part, :], ACROSS, preferred_element_type=jnp.float32
+            )
             yield
 
-    def flush_keys(u):
+    def flush_values(u):
+        s = units[u][0]
+        for c in chunks(u):
+            part = slice(c, c + TILE)
+            vt[s, :, part] += lax.dot_general(
+                turned[u % 3, 1], prob16[u % 2, part, :], ACROSS, preferred_element_type=jnp.float32
+            )
+            yield
+
+    def flush_queries(u, side):
         s, columns = units[u][0], columns_of(u)
-        kt[s, :, 0:columns] += lax.dot_general(
-            turned[u % 3, 0], dscore16[u % 2, 0:columns, :], ACROSS, preferred_element_type=jnp.float32
-        )
-        yield
-
-    def flush_values(u):
-        s, columns = units[u][0], columns_of(u)
-        vt[s, :, 0:columns] += lax.dot_general(
-            turned[u % 3, 1], prob16[u % 2, 0:columns, :], ACROSS, preferred_element_type=jnp.float32
-        )
-        yield
-
-    def flush_queries(u):
-        s, columns = units[u][0], columns_of(u)
-        for side in range(2):
-            ds = dscore16[u % 2, 0:columns, lanes_of(side)]
-            dqt = jnp.dot(keys_t[s, :, 0:columns], ds, preferred_element_type=jnp.float32)
-            for h in range(2):
-                first = (first_head(u, side) + h) * width
-                dq = dqt[:, h * TILE : (h + 1) * TILE].T * score_scale
-                dq_all[rows_of(u), first : first + width] = dq
+        for h in range(2):
+            lanes = slice((2 * side + h) * TILE, (2 * side + h + 1) * TILE)
+            dqt = jnp.dot(
+                keys_t[s, :, 0:columns], dscore16[u % 2, 0:columns, lanes], preferred_element_type=jnp.float32
+            )
+            first = (first_head(u, side) + h) * width
+            dq_all[rows_of(u), first : first + width] = dqt.T * score_scale
             yield
 
     def together(*steps):
-        steps = list(steps)
+        steps = [[generator, count, 0] for generator, count in steps]
         while steps:
-            for step in list(steps):
-                if next(step, steps) is steps:
-                    steps.remove(step)
+            step = min(steps, key=lambda step: (step[2] + 0.5) / step[1])
+            step[2] += 1
+            if next(step[0], steps) is steps:
+                steps.remove(step)
 
     def wait_rows(u):
         s, index, g = units[u]
@@ -326,35 +331,52 @@
     count = len(units)
     per_slot = tiles * groups
     stats = [({}, {}) for _ in units]
-    together(prepare(0))
+
+    def head_step(u, side):
+        return (head(u, side, stats[u][side]), 2 * len(chunks(u)))
+
+    def tail_step(u, side):
+        return (tail(u, side, stats[u][side]), columns_of(u) // PIECE)
+
+    def keys_step(u):
+        return (flush_keys(u), len(chunks(u)))
+
+    def values_step(u):
+        return (flush_values(u), len(chunks(u)))
+
+    def queries_step(u, side):
+        return (flush_queries(u, side), 2)
+
+    together((prepare(0), 3))
     wait_rows(0)
-    together(head(0, 0, stats[0][0]))
+    together(head_step(0, 0))
     for u in range(count):
         s = units[u][0]
-        steps = [head(u, 1, stats[u][1]), tail(u, 0, stats[u][0])]
+        steps = [head_step(u, 1), tail_step(u, 0)]
         if u >= 1:
-            steps += [flush_keys(u - 1), flush_queries(u - 1)]
+            steps += [keys_step(u - 1), queries_step(u - 1, 0)]
         if u % per_slot == 2 and s + 1 < slots:
-            steps.append(prepare(s + 1))
+            steps.append((prepare(s + 1), 3))
         if u % per_slot == 1 and s >= 1:
-            steps.append(finish(s - 1))
+            steps.append((finish(s - 1), 3))
         together(*steps)
-        if u >= 1 and units[u - 1][2] == groups - 1:
-            dq_copy(units[u - 1][0] * tiles + units[u - 1][1]).start()
         if u % per_slot == 1 and s >= 1:
             drk_copy(s - 1).start()
             drv_copy(s - 1).start()
         steps = []
         if u + 1 < count:
             wait_rows(u + 1)
-            steps.append(head(u + 1, 0, stats[u + 1][0]))
-        steps.append(tail(u, 1, stats[u][1]))
+            steps.append(head_step(u + 1, 0))
+        steps.append(tail_step(u, 1))
         if u >= 1:
-            steps.append(flush_values(u - 1))
+            steps += [values_step(u - 1), queries_step(u - 1, 1)]
         together(*steps)
-    together(flush_keys(count - 1), flush_values(count - 1), flush_queries(count - 1))
+        if u >= 1 and units[u - 1][2] == groups - 1:
+            dq_copy(units[u - 1][0] * tiles + units[u - 1][1]).start()
+    last = count - 1
+    together(keys_step(last), values_step(last), queries_step(last, 0), queries_step(last, 1))
     dq_copy(slots * tiles - 1).start()
-    together(finish(slots - 1))
+    together((finish(slots - 1), 3))
     drk_copy(slots - 1).start()
     drv_copy(slots - 1).start()
 

time: 48 us -> 48.1 us (level)
  no operation moved by 1% of the time
where the time goes in v4:
time: 48.1 us; the launch traced here: 47.8 us
  blocking collectives  26.3 us (55%)
  Pallas kernels  14.6 us (30%)
  waiting for transfers between devices  2.94 us (6%)
  other arithmetic  1.73 us (4%)
  local copies, waits for them, and re-layouts  1.27 us (3%)
  between operations  0.65 us (1%)
    all_to_all x2, blocking collectives, exchange(): lax.all_to_all(x, 'seq', split_axis=0, concat_axis=0, axis_index_groups=s...  26.3 us
    pallas_call x1, Pallas kernels, slot_grads(): pl.pallas_call(grad_kernel, in_specs=[hbm] * 10, out_specs=[hbm] * 5, out...  14.6 us
    ppermute x2, waiting for transfers between devices, swap_cores(): return lax.ppermute(x, 'seq', [(i, i ^ 1) for i in range(n)])  2.94 us
    add x1, other arithmetic, body(): parts = exchange(own_term + swap_cores(other_term, n), n)  0.99 us
  transfers between devices with their start and end apart: 2, of which 2 were waited for; matrix products, arithmetic and copies ran while one was open for 0% of the time, Pallas kernels for 0%

profile of v4, /device:TPU:0, one launch (start us, length us, event | category | flops | bytes accessed | tf_op | source)
XLA Modules:
  0.0 47.8 jit_solution(465165911064774941)
XLA Ops:
  0.6 0.7 %pad_add_fusion = bf16[32,256]{1,0:T(8,128)(2,1)S(1)} fusion(bf16[32,128]{1,0:T(8,128)(2,1)} %param.15, bf16[32,128]{1,0:T(8,128)(2,1)} %param.14), kind=kLoop, calls=%fused_computation | loop fusion | flops 32768 | bytes 32768 | tf_op jit(solution)/shard_map/add | solution.py:471
  1.4 14.4 %all_to_all.17 = bf16[8,32,256]{2,1,0:T(8,128)(2,1)S(1)} all-to-all(bf16[8,32,256]{2,1,0:T(8,128)(2,1)S(1)} %broadcast_in_dim.2), channel_id=1, replica_groups={{0,2,4,6,8,10,12,14},{1,3,5,7,9,11,13,15},{16,18,20,22,24,26,28,30},{17..., dimensions={0} | all-to-all | bytes 262144 | tf_op jit(solution)/shard_map/all_to_all | solution.py:30
  15.8 0.0 copy-start
  15.8 0.0 collective-permute-start
  15.8 1.3 %collective-permute-done.other_hbm = bf16[256,256]{1,0:T(8,128)(2,1)S(1)} collective-permute-done((bf16[256,256]{1,0:T(8,128)(2,1)S(1)}, bf16[256,256]{1,0:T(8,128)(2,1)S(1)}, u32[]{:S(2)}, u32[]{:S(2)}) %collective-permute-start) | collective-permute-done | bytes 131104 | tf_op jit(solution)/shard_map/ppermute | solution.py:26
  17.1 0.0 copy-done
  17.1 0.0 copy-start.1
  17.1 0.6 %copy-done.1 = bf16[256,256]{1,0:T(8,128)(2,1)} copy-done((bf16[256,256]{1,0:T(8,128)(2,1)}, bf16[256,256]{1,0:T(8,128)(2,1)S(1)}, u32[]{:S(2)}) %copy-start.1) | copy-done | bytes 131096
  17.8 14.6 %shard_map.137 = (f32[768,1024]{1,0:T(8,128)}, f32[768,128]{1,0:T(8,128)}, f32[768,128]{1,0:T(8,128)}, f32[256,256]{1,0:T(8,128)}, f32[256,256]{1,0:T(8,128)}) custom-call(s32[2]{0:T(128)} %prompt_hbm.1, s32[2]{0:T(128)} %length_hbm.1, s32[2]{0:T(128)} %begin_hbm.1, s32[16]{0:T(128)} %holder_hbm.1, bf16[768,1024]{1,0:T(8,128)(2,1)} %q_hbm.1, ...), custom_call_target="tpu_custom_call" | custom-call | tf_op jit(solution)/shard_map/pallas_call | solution.py:404
  32.4 0.2 collective-permute-start.1
  32.6 1.6 %collective-permute-done.1 = f32[256,256]{1,0:T(8,128)S(1)} collective-permute-done((f32[256,256]{1,0:T(8,128)}, f32[256,256]{1,0:T(8,128)S(1)}, u32[]{:S(2)}, u32[]{:S(2)}) %collective-permute-start.1) | collective-permute-done | bytes 262176 | tf_op jit(solution)/shard_map/ppermute | solution.py:26
  34.2 1.0 %add.11 = f32[256,256]{1,0:T(8,128)S(1)} add(f32[256,256]{1,0:T(8,128)} %get-tuple-element.13, f32[256,256]{1,0:T(8,128)S(1)} %collective-permute-done.1) | non-fusion elementwise | flops 65536 | bytes 786432 | tf_op jit(solution)/shard_map/add | solution.py:479
  35.2 11.9 %all_to_all.18 = f32[8,32,256]{2,1,0:T(8,128)S(1)} all-to-all(f32[8,32,256]{2,1,0:T(8,128)S(1)} %bitcast.2), channel_id=1, replica_groups={{0,2,4,6,8,10,12,14},{1,3,5,7,9,11,13,15},{16,18,20,22,24,26,28,30},{17..., dimensions={0} | all-to-all | bytes 524288 | tf_op jit(solution)/shard_map/all_to_all | solution.py:30
  47.2 0.6 %fusion = (f32[32,128]{1,0:T(8,128)}, f32[32,128]{1,0:T(8,128)}) fusion(f32[32,256]{1,0:T(8,128)S(1)} %reduce_sum.9), kind=kLoop, calls=%fused_computation.1 | loop fusion | bytes 65536 | tf_op jit(solution)/shard_map/slice | solution.py:481
  (2 shorter events, 0.0 us)
Async XLA Ops:
  15.8 1.4 %copy-start = (bf16[8,32,256]{2,1,0:T(8,128)(2,1)}, bf16[8,32,256]{2,1,0:T(8,128)(2,1)S(1)}, u32[]{:S(2)}) copy-start(bf16[8,32,256]{2,1,0:T(8,128)(2,1)S(1)} %all_to_all.17) | copy-start | bytes 393220
  15.8 1.3 %collective-permute-start = (bf16[256,256]{1,0:T(8,128)(2,1)S(1)}, bf16[256,256]{1,0:T(8,128)(2,1)S(1)}, u32[]{:S(2)}, u32[]{:S(2)}) collective-permute-start(bf16[256,256]{1,0:T(8,128)(2,1)S(1)} %bitcast.3), channel_id=1, source_target_pairs={{0,1},{1,0},{2,3},{3,2},{4,5},{5,4},{6,7},{7,6},{8,9},{9,8},{10,11... | collective-permute-start | bytes 393224 | tf_op jit(solution)/shard_map/ppermute | solution.py:26
  17.1 0.6 %copy-start.1 = (bf16[256,256]{1,0:T(8,128)(2,1)}, bf16[256,256]{1,0:T(8,128)(2,1)S(1)}, u32[]{:S(2)}) copy-start(bf16[256,256]{1,0:T(8,128)(2,1)S(1)} %collective-permute-done.other_hbm) | copy-start | bytes 393220
  32.4 1.8 %collective-permute-start.1 = (f32[256,256]{1,0:T(8,128)}, f32[256,256]{1,0:T(8,128)S(1)}, u32[]{:S(2)}, u32[]{:S(2)}) collective-permute-start(f32[256,256]{1,0:T(8,128)} %get-tuple-element.14), channel_id=1, source_target_pairs={{0,1},{1,0},{2,3},{3,2},{4,5},{5,4},{6,7},{7,6},{8,9},{9,8},{10,11... | collective-permute-start | bytes 786440 | tf_op jit(solution)/shard_map/ppermute | solution.py:26

commit v5 on v3

--- a/solution.py
+++ b/solution.py
@@ -10,6 +10,7 @@
 
 OWNERS = 8
 TILE = 128
+ROWS = 64
 PIECE = 16
 score_scale = 0.08838834764831845
 EXP2_SCALE = score_scale * math.log2(math.e)
@@ -153,50 +154,61 @@
     ]
     for copy in scalar_copies + kv_copies + resp_copies:
         copy.start()
-    for chunk in range(slots * tiles):
-        q_copy(chunk).start()
-        g_copy(chunk).start()
+    q_copy(0).start()
+    g_copy(0).start()
 
     term_ref[...] = jnp.zeros_like(term_ref)
     causal_bias[...] = jnp.where(
-        lax.broadcasted_iota(jnp.int32, (TILE, TILE), 0)
-        <= lax.broadcasted_iota(jnp.int32, (TILE, TILE), 1),
+        lax.broadcasted_iota(jnp.int32, causal_bias.shape, 0)
+        <= (lax.broadcasted_iota(jnp.int32, causal_bias.shape, 1) & (ROWS - 1)),
         0.0,
         MASKED,
     )
     for copy in scalar_copies + kv_copies + resp_copies:
         copy.wait()
 
+    for chunk in range(1, slots * tiles):
+        q_copy(chunk).start()
+        g_copy(chunk).start()
+
     @pl.loop(0, n)
     def _(j):
         place[holder_ref[j]] = j
 
     wide = 2 * TILE
-    at_once = 4
-    groups = heads // at_once
-    units = [(s, index, g) for s in range(slots) for index in range(tiles) for g in range(groups)]
+    at_once = wide // ROWS
+    steps_of = slot_rows // ROWS
+    units = []
+    for s in range(slots):
+        order = range(steps_of) if s + 1 < slots else range(steps_of - 1, -1, -1)
+        units += [(s, index) for index in order]
 
     def columns_of(u):
-        return prompt_len + (units[u][1] + 1) * TILE
+        return prompt_len + (units[u][1] + 1) * ROWS
+
+    def padded_columns(u):
+        return -(-columns_of(u) // TILE) * TILE
 
     def rows_of(u):
-        s, index, _ = units[u]
-        first = (s * tiles + index) * TILE
-        return slice(first, first + TILE)
-
-    def first_head(u, side):
-        return units[u][2] * at_once + 2 * side
+        s, index = units[u]
+        first = s * slot_rows + index * ROWS
+        return slice(first, first + ROWS)
+
+    def chunk_of(u):
+        return rows_of(u).start // TILE
 
     def chunks(u):
-        return range(0, columns_of(u), TILE)
+        columns = columns_of(u)
+        return [(c, min(TILE, columns - c)) for c in range(0, columns, TILE)]
 
     def lanes_of(side):
         return slice(side * wide, (side + 1) * wide)
 
     def stacked(ref, u, side):
-        first = first_head(u, side)
+        first = side * at_once
         return jnp.concatenate(
-            [ref[rows_of(u), (first + h) * width : (first + h + 1) * width] for h in range(2)], axis=0
+            [ref[rows_of(u), (first + h) * width : (first + h + 1) * width] for h in range(at_once)],
+            axis=0,
         )
 
     def fold(x, how):
@@ -239,7 +251,7 @@
         yield
 
     def head(u, side, out):
-        s, index, _ = units[u]
+        s, index = units[u]
         columns, buf = columns_of(u), u % 2
         q2t, g2t = turned.at[u % 3, 0, :, lanes_of(side)], turned.at[u % 3, 1, :, lanes_of(side)]
         q2t[...] = stacked(q_all, u, side).T
@@ -247,13 +259,14 @@
         tops, totals, weights = [], [], []
         all_scores = jnp.dot(keys[s, 0:columns, :], q2t[...], preferred_element_type=jnp.float32)
         all_dprobs = jnp.dot(values[s, 0:columns, :], g2t[...], preferred_element_type=jnp.float32)
-        for c in chunks(u):
-            part = slice(c, c + TILE)
+        for c, size in chunks(u):
+            part = slice(c, c + size)
             block = all_scores[part]
             if c >= prompt_len:
-                bias = live_bias[s, c - prompt_len : c - prompt_len + TILE, :]
-                if c + TILE == columns:
-                    bias = bias + causal_bias[...]
+                bias = live_bias[s, c - prompt_len : c - prompt_len + size, :]
+                if c + size == columns:
+                    last = bias[size - ROWS :] + causal_bias[...]
+                    bias = last if size == ROWS else jnp.concatenate([bias[: size - ROWS], last], axis=0)
                 block = block + jnp.concatenate([bias, bias], axis=1)
             top = fold(block, jnp.max) * EXP2_SCALE
             e = jnp.exp2(block * EXP2_SCALE - top)
@@ -269,47 +282,53 @@
         factors = [jnp.exp2(part - top) for part in tops]
         total = functools.reduce(jnp.add, [f * x for f, x in zip(factors, totals)])
         weighted = functools.reduce(jnp.add, [f * x for f, x in zip(factors, weights)])
-        row = index * TILE + lax.broadcasted_iota(jnp.int32, (1, TILE), 1)
+        row = index * ROWS + (lax.broadcasted_iota(jnp.int32, (1, wide), 1) & (ROWS - 1))
         live = (row >= begin_ref[s]) & (row < begin_ref[s] + length_ref[s])
-        inverse = jnp.where(jnp.concatenate([live, live], axis=1), 1.0 / total, 0.0)
+        inverse = jnp.where(live, 1.0 / total, 0.0)
         out["delta"] = weighted * inverse
         out["factors"] = [f * inverse for f in factors]
 
     def tail(u, side, stats):
         buf, lanes = u % 2, lanes_of(side)
         delta = stats["delta"]
-        for c, factor in zip(chunks(u), stats["factors"]):
-            for first in range(c, c + TILE, PIECE):
+        for (c, size), factor in zip(chunks(u), stats["factors"]):
+            for first in range(c, c + size, PIECE):
                 part = slice(first, first + PIECE)
                 p = exps[buf, side, part, :] * factor
                 prob16[buf, part, lanes] = p.astype(jnp.bfloat16)
                 ds = p * (dprobs[buf, side, part, :] - delta)
                 dscore16[buf, part, lanes] = ds.astype(jnp.bfloat16)
             yield
+        pad = slice(columns_of(u), padded_columns(u))
+        if pad.start < pad.stop:
+            zero = jnp.zeros((pad.stop - pad.start, wide), jnp.bfloat16)
+            prob16[buf, pad, lanes] = zero
+            dscore16[buf, pad, lanes] = zero
+            yield
 
     def flush_keys(u):
-        s, columns = units[u][0], columns_of(u)
+        s, columns = units[u][0], padded_columns(u)
         kt[s, :, 0:columns] += lax.dot_general(
             turned[u % 3, 0], dscore16[u % 2, 0:columns, :], ACROSS, preferred_element_type=jnp.float32
         )
         yield
 
     def flush_values(u):
-        s, columns = units[u][0], columns_of(u)
+        s, columns = units[u][0], padded_columns(u)
         vt[s, :, 0:columns] += lax.dot_general(
             turned[u % 3, 1], prob16[u % 2, 0:columns, :], ACROSS, preferred_element_type=jnp.float32
         )
         yield
 
     def flush_queries(u):
-        s, columns = units[u][0], columns_of(u)
+        s, columns = units[u][0], padded_columns(u)
         for side in range(2):
             ds = dscore16[u % 2, 0:columns, lanes_of(side)]
             dqt = jnp.dot(keys_t[s, :, 0:columns], ds, preferred_element_type=jnp.float32)
-            for h in range(2):
-                first = (first_head(u, side) + h) * width
-                dq = dqt[:, h * TILE : (h + 1) * TILE].T * score_scale
-                dq_all[rows_of(u), first : first + width] = dq
+            dq = dqt.T * score_scale
+            for h in range(at_once):
+                first = (side * at_once + h) * width
+                dq_all[rows_of(u), first : first + width] = dq[h * ROWS : (h + 1) * ROWS]
             yield
 
     def together(*steps):
@@ -320,13 +339,16 @@
                     steps.remove(step)
 
     def wait_rows(u):
-        s, index, g = units[u]
-        if g == 0:
-            q_copy(s * tiles + index).wait()
-            g_copy(s * tiles + index).wait()
+        if all(chunk_of(other) != chunk_of(u) for other in range(u)):
+            q_copy(chunk_of(u)).wait()
+            g_copy(chunk_of(u)).wait()
+
+    def send_rows(u):
+        if all(chunk_of(other) != chunk_of(u) for other in range(u + 1, len(units))):
+            dq_copy(chunk_of(u)).start()
 
     count = len(units)
-    per_slot = tiles * groups
+    per_slot = steps_of
     stats = [({}, {}) for _ in units]
     together(prepare(0))
     wait_rows(0)
@@ -341,8 +363,8 @@
         if u % per_slot == 1 and s >= 1:
             steps.append(finish(s - 1))
         together(*steps)
-        if u >= 1 and units[u - 1][2] == groups - 1:
-            dq_copy(units[u - 1][0] * tiles + units[u - 1][1]).start()
+        if u >= 1:
+            send_rows(u - 1)
         if u % per_slot == 1 and s >= 1:
             drk_copy(s - 1).start()
             drv_copy(s - 1).start()
@@ -355,7 +377,7 @@
             steps.append(flush_values(u - 1))
         together(*steps)
     together(flush_keys(count - 1), flush_values(count - 1), flush_queries(count - 1))
-    dq_copy(slots * tiles - 1).start()
+    send_rows(count - 1)
     together(finish(slots - 1))
     drk_copy(slots - 1).start()
     drv_copy(slots - 1).start()
@@ -411,7 +433,7 @@
             pltpu.VMEM((slots, total, width), bf16),
             pltpu.VMEM((slots, width, total), bf16),
             pltpu.VMEM((slots, slot_rows, TILE), f32),
-            pltpu.VMEM((TILE, TILE), f32),
+            pltpu.VMEM((ROWS, TILE), f32),
             pltpu.VMEM((3, 2, width, 4 * TILE), bf16),
             pltpu.VMEM((2, 2, total, 2 * TILE), f32),
             pltpu.VMEM((2, 2, total, 2 * TILE), f32),

time: 48.1 us -> 46.8 us (0.973)
  Pallas kernels: 14.6 us -> 13.3 us
    pallas_call x1, Pallas kernels: 14.6 us -> 13.3 us  [slot_grads(): pl.pallas_call(grad_kernel, in_specs=[hbm] * 10, out_specs=[hbm] * 5, out...]
where the time goes in v5:
time: 46.8 us; the launch traced here: 46.4 us
  blocking collectives  26.3 us (56%)
  Pallas kernels  13.3 us (28%)
  waiting for transfers between devices  2.94 us (6%)
  other arithmetic  1.73 us (4%)
  local copies, waits for them, and re-layouts  1.27 us (3%)
  between operations  0.65 us (1%)
    all_to_all x2, blocking collectives, exchange(): lax.all_to_all(x, 'seq', split_axis=0, concat_axis=0, axis_index_groups=s...  26.3 us
    pallas_call x1, Pallas kernels, slot_grads(): pl.pallas_call(grad_kernel, in_specs=[hbm] * 10, out_specs=[hbm] * 5, out...  13.3 us
    ppermute x2, waiting for transfers between devices, swap_cores(): return lax.ppermute(x, 'seq', [(i, i ^ 1) for i in range(n)])  2.94 us
    add x1, other arithmetic, body(): parts = exchange(own_term + swap_cores(other_term, n), n)  0.99 us
  transfers between devices with their start and end apart: 2, of which 2 were waited for; matrix products, arithmetic and copies ran while one was open for 0% of the time, Pallas kernels for 0%

profile of v5, /device:TPU:0, one launch (start us, length us, event | category | flops | bytes accessed | tf_op | source)
XLA Modules:
  0.0 46.4 jit_solution(10878430596109855143)
XLA Ops:
  0.6 0.7 %pad_add_fusion = bf16[32,256]{1,0:T(8,128)(2,1)S(1)} fusion(bf16[32,128]{1,0:T(8,128)(2,1)} %param.15, bf16[32,128]{1,0:T(8,128)(2,1)} %param.14), kind=kLoop, calls=%fused_computation | loop fusion | flops 32768 | bytes 32768 | tf_op jit(solution)/shard_map/add | solution.py:473
  1.4 14.4 %all_to_all.17 = bf16[8,32,256]{2,1,0:T(8,128)(2,1)S(1)} all-to-all(bf16[8,32,256]{2,1,0:T(8,128)(2,1)S(1)} %broadcast_in_dim.2), channel_id=1, replica_groups={{0,2,4,6,8,10,12,14},{1,3,5,7,9,11,13,15},{16,18,20,22,24,26,28,30},{17..., dimensions={0} | all-to-all | bytes 262144 | tf_op jit(solution)/shard_map/all_to_all | solution.py:31
  15.8 0.0 copy-start
  15.8 0.0 collective-permute-start
  15.8 1.3 %collective-permute-done.other_hbm = bf16[256,256]{1,0:T(8,128)(2,1)S(1)} collective-permute-done((bf16[256,256]{1,0:T(8,128)(2,1)S(1)}, bf16[256,256]{1,0:T(8,128)(2,1)S(1)}, u32[]{:S(2)}, u32[]{:S(2)}) %collective-permute-start) | collective-permute-done | bytes 131104 | tf_op jit(solution)/shard_map/ppermute | solution.py:27
  17.1 0.0 copy-done
  17.1 0.0 copy-start.1
  17.1 0.6 %copy-done.1 = bf16[256,256]{1,0:T(8,128)(2,1)} copy-done((bf16[256,256]{1,0:T(8,128)(2,1)}, bf16[256,256]{1,0:T(8,128)(2,1)S(1)}, u32[]{:S(2)}) %copy-start.1) | copy-done | bytes 131096
  17.8 13.3 %shard_map.137 = (f32[768,1024]{1,0:T(8,128)}, f32[768,128]{1,0:T(8,128)}, f32[768,128]{1,0:T(8,128)}, f32[256,256]{1,0:T(8,128)}, f32[256,256]{1,0:T(8,128)}) custom-call(s32[2]{0:T(128)} %prompt_hbm.1, s32[2]{0:T(128)} %length_hbm.1, s32[2]{0:T(128)} %begin_hbm.1, s32[16]{0:T(128)} %holder_hbm.1, bf16[768,1024]{1,0:T(8,128)(2,1)} %q_hbm.1, ...), custom_call_target="tpu_custom_call" | custom-call | tf_op jit(solution)/shard_map/pallas_call | solution.py:406
  31.1 0.2 collective-permute-start.1
  31.3 1.6 %collective-permute-done.1 = f32[256,256]{1,0:T(8,128)S(1)} collective-permute-done((f32[256,256]{1,0:T(8,128)}, f32[256,256]{1,0:T(8,128)S(1)}, u32[]{:S(2)}, u32[]{:S(2)}) %collective-permute-start.1) | collective-permute-done | bytes 262176 | tf_op jit(solution)/shard_map/ppermute | solution.py:27
  32.9 1.0 %add.11 = f32[256,256]{1,0:T(8,128)S(1)} add(f32[256,256]{1,0:T(8,128)} %get-tuple-element.13, f32[256,256]{1,0:T(8,128)S(1)} %collective-permute-done.1) | non-fusion elementwise | flops 65536 | bytes 786432 | tf_op jit(solution)/shard_map/add | solution.py:481
  33.9 11.9 %all_to_all.18 = f32[8,32,256]{2,1,0:T(8,128)S(1)} all-to-all(f32[8,32,256]{2,1,0:T(8,128)S(1)} %bitcast.2), channel_id=1, replica_groups={{0,2,4,6,8,10,12,14},{1,3,5,7,9,11,13,15},{16,18,20,22,24,26,28,30},{17..., dimensions={0} | all-to-all | bytes 524288 | tf_op jit(solution)/shard_map/all_to_all | solution.py:31
  45.8 0.6 %fusion = (f32[32,128]{1,0:T(8,128)}, f32[32,128]{1,0:T(8,128)}) fusion(f32[32,256]{1,0:T(8,128)S(1)} %reduce_sum.9), kind=kLoop, calls=%fused_computation.1 | loop fusion | bytes 65536 | tf_op jit(solution)/shard_map/slice | solution.py:483
  (2 shorter events, 0.0 us)
Async XLA Ops:
  15.8 1.4 %copy-start = (bf16[8,32,256]{2,1,0:T(8,128)(2,1)}, bf16[8,32,256]{2,1,0:T(8,128)(2,1)S(1)}, u32[]{:S(2)}) copy-start(bf16[8,32,256]{2,1,0:T(8,128)(2,1)S(1)} %all_to_all.17) | copy-start | bytes 393220
  15.8 1.3 %collective-permute-start = (bf16[256,256]{1,0:T(8,128)(2,1)S(1)}, bf16[256,256]{1,0:T(8,128)(2,1)S(1)}, u32[]{:S(2)}, u32[]{:S(2)}) collective-permute-start(bf16[256,256]{1,0:T(8,128)(2,1)S(1)} %bitcast.3), channel_id=1, source_target_pairs={{0,1},{1,0},{2,3},{3,2},{4,5},{5,4},{6,7},{7,6},{8,9},{9,8},{10,11... | collective-permute-start | bytes 393224 | tf_op jit(solution)/shard_map/ppermute | solution.py:27
  17.1 0.6 %copy-start.1 = (bf16[256,256]{1,0:T(8,128)(2,1)}, bf16[256,256]{1,0:T(8,128)(2,1)S(1)}, u32[]{:S(2)}) copy-start(bf16[256,256]{1,0:T(8,128)(2,1)S(1)} %collective-permute-done.other_hbm) | copy-start | bytes 393220
  31.1 1.8 %collective-permute-start.1 = (f32[256,256]{1,0:T(8,128)}, f32[256,256]{1,0:T(8,128)S(1)}, u32[]{:S(2)}, u32[]{:S(2)}) collective-permute-start(f32[256,256]{1,0:T(8,128)} %get-tuple-element.14), channel_id=1, source_target_pairs={{0,1},{1,0},{2,3},{3,2},{4,5},{5,4},{6,7},{7,6},{8,9},{9,8},{10,11... | collective-permute-start | bytes 786440 | tf_op jit(solution)/shard_map/ppermute | solution.py:27

commit v6 on v5

--- a/solution.py
+++ b/solution.py
@@ -11,6 +11,7 @@
 OWNERS = 8
 TILE = 128
 ROWS = 64
+SPAN = 64
 PIECE = 16
 score_scale = 0.08838834764831845
 EXP2_SCALE = score_scale * math.log2(math.e)
@@ -199,7 +200,7 @@
 
     def chunks(u):
         columns = columns_of(u)
-        return [(c, min(TILE, columns - c)) for c in range(0, columns, TILE)]
+        return [(c, min(SPAN, columns - c)) for c in range(0, columns, SPAN)]
 
     def lanes_of(side):
         return slice(side * wide, (side + 1) * wide)
@@ -211,8 +212,8 @@
             axis=0,
         )
 
-    def fold(x, how):
-        return how(how(x.reshape(x.shape[0] // 8, 8, x.shape[1]), axis=0), axis=0, keepdims=True)
+    def classes(x):
+        return x.reshape(x.shape[0] // 8, 8, x.shape[1])
 
     def prepare(s):
         first_block = prompt_ref[s] * OWNERS
@@ -268,20 +269,23 @@
                     last = bias[size - ROWS :] + causal_bias[...]
                     bias = last if size == ROWS else jnp.concatenate([bias[: size - ROWS], last], axis=0)
                 block = block + jnp.concatenate([bias, bias], axis=1)
-            top = fold(block, jnp.max) * EXP2_SCALE
-            e = jnp.exp2(block * EXP2_SCALE - top)
-            exps[buf, side, part, :] = e
+            block = classes(block)
+            top = jnp.max(block, axis=0) * EXP2_SCALE
+            e = jnp.exp2(block * EXP2_SCALE - top[None])
+            exps[buf, side, part, :] = e.reshape(size, wide)
             yield
             d = all_dprobs[part]
             dprobs[buf, side, part, :] = d
             tops.append(top)
-            totals.append(fold(e, jnp.sum))
-            weights.append(fold(e * d, jnp.sum))
+            totals.append(jnp.sum(e, axis=0))
+            weights.append(jnp.sum(e * classes(d), axis=0))
             yield
-        top = functools.reduce(jnp.maximum, tops)
+        top = jnp.max(functools.reduce(jnp.maximum, tops), axis=0, keepdims=True)
         factors = [jnp.exp2(part - top) for part in tops]
         total = functools.reduce(jnp.add, [f * x for f, x in zip(factors, totals)])
         weighted = functools.reduce(jnp.add, [f * x for f, x in zip(factors, weights)])
+        total = jnp.sum(total, axis=0, keepdims=True)
+        weighted = jnp.sum(weighted, axis=0, keepdims=True)
         row = index * ROWS + (lax.broadcasted_iota(jnp.int32, (1, wide), 1) & (ROWS - 1))
         live = (row >= begin_ref[s]) & (row < begin_ref[s] + length_ref[s])
         inverse = jnp.where(live, 1.0 / total, 0.0)
@@ -294,7 +298,7 @@
         for (c, size), factor in zip(chunks(u), stats["factors"]):
             for first in range(c, c + size, PIECE):
                 part = slice(first, first + PIECE)
-                p = exps[buf, side, part, :] * factor
+                p = (classes(exps[buf, side, part, :]) * factor[None]).reshape(PIECE, wide)
                 prob16[buf, part, lanes] = p.astype(jnp.bfloat16)
                 ds = p * (dprobs[buf, side, part, :] - delta)
                 dscore16[buf, part, lanes] = ds.astype(jnp.bfloat16)

time: 46.8 us -> 46.1 us (0.985)
  Pallas kernels: 13.3 us -> 12.6 us
    pallas_call x1, Pallas kernels: 13.3 us -> 12.6 us  [slot_grads(): pl.pallas_call(grad_kernel, in_specs=[hbm] * 10, out_specs=[hbm] * 5, out...]
where the time goes in v6:
time: 46.1 us; the launch traced here: 45.8 us
  blocking collectives  26.3 us (57%)
  Pallas kernels  12.6 us (27%)
  waiting for transfers between devices  2.94 us (6%)
  other arithmetic  1.73 us (4%)
  local copies, waits for them, and re-layouts  1.27 us (3%)
  between operations  0.65 us (1%)
    all_to_all x2, blocking collectives, exchange(): lax.all_to_all(x, 'seq', split_axis=0, concat_axis=0, axis_index_groups=s...  26.3 us
    pallas_call x1, Pallas kernels, slot_grads(): pl.pallas_call(grad_kernel, in_specs=[hbm] * 10, out_specs=[hbm] * 5, out...  12.6 us
    ppermute x2, waiting for transfers between devices, swap_cores(): return lax.ppermute(x, 'seq', [(i, i ^ 1) for i in range(n)])  2.94 us
    add x1, other arithmetic, body(): parts = exchange(own_term + swap_cores(other_term, n), n)  0.99 us
  transfers between devices with their start and end apart: 2, of which 2 were waited for; matrix products, arithmetic and copies ran while one was open for 0% of the time, Pallas kernels for 0%

profile of v6, /device:TPU:0, one launch (start us, length us, event | category | flops | bytes accessed | tf_op | source)
XLA Modules:
  0.0 45.8 jit_solution(9540308174465848741)
XLA Ops:
  0.6 0.7 %pad_add_fusion = bf16[32,256]{1,0:T(8,128)(2,1)S(1)} fusion(bf16[32,128]{1,0:T(8,128)(2,1)} %param.15, bf16[32,128]{1,0:T(8,128)(2,1)} %param.14), kind=kLoop, calls=%fused_computation | loop fusion | flops 32768 | bytes 32768 | tf_op jit(solution)/shard_map/add | solution.py:477
  1.4 14.4 %all_to_all.17 = bf16[8,32,256]{2,1,0:T(8,128)(2,1)S(1)} all-to-all(bf16[8,32,256]{2,1,0:T(8,128)(2,1)S(1)} %broadcast_in_dim.2), channel_id=1, replica_groups={{0,2,4,6,8,10,12,14},{1,3,5,7,9,11,13,15},{16,18,20,22,24,26,28,30},{17..., dimensions={0} | all-to-all | bytes 262144 | tf_op jit(solution)/shard_map/all_to_all | solution.py:32
  15.8 0.0 copy-start
  15.8 0.0 collective-permute-start
  15.8 1.3 %collective-permute-done.other_hbm = bf16[256,256]{1,0:T(8,128)(2,1)S(1)} collective-permute-done((bf16[256,256]{1,0:T(8,128)(2,1)S(1)}, bf16[256,256]{1,0:T(8,128)(2,1)S(1)}, u32[]{:S(2)}, u32[]{:S(2)}) %collective-permute-start) | collective-permute-done | bytes 131104 | tf_op jit(solution)/shard_map/ppermute | solution.py:28
  17.1 0.0 copy-done
  17.1 0.0 copy-start.1
  17.1 0.6 %copy-done.1 = bf16[256,256]{1,0:T(8,128)(2,1)} copy-done((bf16[256,256]{1,0:T(8,128)(2,1)}, bf16[256,256]{1,0:T(8,128)(2,1)S(1)}, u32[]{:S(2)}) %copy-start.1) | copy-done | bytes 131096
  17.8 12.6 %shard_map.137 = (f32[768,1024]{1,0:T(8,128)}, f32[768,128]{1,0:T(8,128)}, f32[768,128]{1,0:T(8,128)}, f32[256,256]{1,0:T(8,128)}, f32[256,256]{1,0:T(8,128)}) custom-call(s32[2]{0:T(128)} %prompt_hbm.1, s32[2]{0:T(128)} %length_hbm.1, s32[2]{0:T(128)} %begin_hbm.1, s32[16]{0:T(128)} %holder_hbm.1, bf16[768,1024]{1,0:T(8,128)(2,1)} %q_hbm.1, ...), custom_call_target="tpu_custom_call" | custom-call | tf_op jit(solution)/shard_map/pallas_call | solution.py:410
  30.4 0.2 collective-permute-start.1
  30.7 1.6 %collective-permute-done.1 = f32[256,256]{1,0:T(8,128)S(1)} collective-permute-done((f32[256,256]{1,0:T(8,128)}, f32[256,256]{1,0:T(8,128)S(1)}, u32[]{:S(2)}, u32[]{:S(2)}) %collective-permute-start.1) | collective-permute-done | bytes 262176 | tf_op jit(solution)/shard_map/ppermute | solution.py:28
  32.3 1.0 %add.11 = f32[256,256]{1,0:T(8,128)S(1)} add(f32[256,256]{1,0:T(8,128)} %get-tuple-element.13, f32[256,256]{1,0:T(8,128)S(1)} %collective-permute-done.1) | non-fusion elementwise | flops 65536 | bytes 786432 | tf_op jit(solution)/shard_map/add | solution.py:485
  33.2 11.9 %all_to_all.18 = f32[8,32,256]{2,1,0:T(8,128)S(1)} all-to-all(f32[8,32,256]{2,1,0:T(8,128)S(1)} %bitcast.2), channel_id=1, replica_groups={{0,2,4,6,8,10,12,14},{1,3,5,7,9,11,13,15},{16,18,20,22,24,26,28,30},{17..., dimensions={0} | all-to-all | bytes 524288 | tf_op jit(solution)/shard_map/all_to_all | solution.py:32
  45.2 0.6 %fusion = (f32[32,128]{1,0:T(8,128)}, f32[32,128]{1,0:T(8,128)}) fusion(f32[32,256]{1,0:T(8,128)S(1)} %reduce_sum.9), kind=kLoop, calls=%fused_computation.1 | loop fusion | bytes 65536 | tf_op jit(solution)/shard_map/slice | solution.py:487
  (2 shorter events, 0.0 us)
Async XLA Ops:
  15.8 1.4 %copy-start = (bf16[8,32,256]{2,1,0:T(8,128)(2,1)}, bf16[8,32,256]{2,1,0:T(8,128)(2,1)S(1)}, u32[]{:S(2)}) copy-start(bf16[8,32,256]{2,1,0:T(8,128)(2,1)S(1)} %all_to_all.17) | copy-start | bytes 393220
  15.8 1.3 %collective-permute-start = (bf16[256,256]{1,0:T(8,128)(2,1)S(1)}, bf16[256,256]{1,0:T(8,128)(2,1)S(1)}, u32[]{:S(2)}, u32[]{:S(2)}) collective-permute-start(bf16[256,256]{1,0:T(8,128)(2,1)S(1)} %bitcast.3), channel_id=1, source_target_pairs={{0,1},{1,0},{2,3},{3,2},{4,5},{5,4},{6,7},{7,6},{8,9},{9,8},{10,11... | collective-permute-start | bytes 393224 | tf_op jit(solution)/shard_map/ppermute | solution.py:28
  17.1 0.6 %copy-start.1 = (bf16[256,256]{1,0:T(8,128)(2,1)}, bf16[256,256]{1,0:T(8,128)(2,1)S(1)}, u32[]{:S(2)}) copy-start(bf16[256,256]{1,0:T(8,128)(2,1)S(1)} %collective-permute-done.other_hbm) | copy-start | bytes 393220
  30.4 1.8 %collective-permute-start.1 = (f32[256,256]{1,0:T(8,128)}, f32[256,256]{1,0:T(8,128)S(1)}, u32[]{:S(2)}, u32[]{:S(2)}) collective-permute-start(f32[256,256]{1,0:T(8,128)} %get-tuple-element.14), channel_id=1, source_target_pairs={{0,1},{1,0},{2,3},{3,2},{4,5},{5,4},{6,7},{7,6},{8,9},{9,8},{10,11... | collective-permute-start | bytes 786440 | tf_op jit(solution)/shard_map/ppermute | solution.py:28

commit v7 on v6

--- a/solution.py
+++ b/solution.py
@@ -11,6 +11,7 @@
 OWNERS = 8
 TILE = 128
 ROWS = 64
+SIDE = 32
 SPAN = 64
 PIECE = 16
 score_scale = 0.08838834764831845
@@ -161,7 +162,7 @@
     term_ref[...] = jnp.zeros_like(term_ref)
     causal_bias[...] = jnp.where(
         lax.broadcasted_iota(jnp.int32, causal_bias.shape, 0)
-        <= (lax.broadcasted_iota(jnp.int32, causal_bias.shape, 1) & (ROWS - 1)),
+        <= (lax.broadcasted_iota(jnp.int32, causal_bias.shape, 1) & (SIDE - 1)),
         0.0,
         MASKED,
     )
@@ -177,18 +178,18 @@
         place[holder_ref[j]] = j
 
     wide = 2 * TILE
-    at_once = wide // ROWS
+    at_once = wide // SIDE
     steps_of = slot_rows // ROWS
     units = []
     for s in range(slots):
         order = range(steps_of) if s + 1 < slots else range(steps_of - 1, -1, -1)
         units += [(s, index) for index in order]
 
-    def columns_of(u):
-        return prompt_len + (units[u][1] + 1) * ROWS
+    def columns_of(u, side):
+        return prompt_len + units[u][1] * ROWS + (side + 1) * SIDE
 
     def padded_columns(u):
-        return -(-columns_of(u) // TILE) * TILE
+        return -(-columns_of(u, 1) // TILE) * TILE
 
     def rows_of(u):
         s, index = units[u]
@@ -198,19 +199,20 @@
     def chunk_of(u):
         return rows_of(u).start // TILE
 
-    def chunks(u):
-        columns = columns_of(u)
+    def chunks(u, side):
+        columns = columns_of(u, side)
         return [(c, min(SPAN, columns - c)) for c in range(0, columns, SPAN)]
 
     def lanes_of(side):
         return slice(side * wide, (side + 1) * wide)
 
+    def side_rows(u, side):
+        first = rows_of(u).start + side * SIDE
+        return slice(first, first + SIDE)
+
     def stacked(ref, u, side):
-        first = side * at_once
-        return jnp.concatenate(
-            [ref[rows_of(u), (first + h) * width : (first + h + 1) * width] for h in range(at_once)],
-            axis=0,
-        )
+        part = side_rows(u, side)
+        return jnp.concatenate([ref[part, h * width : (h + 1) * width] for h in range(at_once)], axis=0)
 
     def classes(x):
         return x.reshape(x.shape[0] // 8, 8, x.shape[1])
@@ -253,21 +255,21 @@
 
     def head(u, side, out):
         s, index = units[u]
-        columns, buf = columns_of(u), u % 2
+        columns, buf = columns_of(u, side), u % 2
         q2t, g2t = turned.at[u % 3, 0, :, lanes_of(side)], turned.at[u % 3, 1, :, lanes_of(side)]
         q2t[...] = stacked(q_all, u, side).T
         g2t[...] = stacked(g_all, u, side).T
         tops, totals, weights = [], [], []
         all_scores = jnp.dot(keys[s, 0:columns, :], q2t[...], preferred_element_type=jnp.float32)
         all_dprobs = jnp.dot(values[s, 0:columns, :], g2t[...], preferred_element_type=jnp.float32)
-        for c, size in chunks(u):
+        for c, size in chunks(u, side):
             part = slice(c, c + size)
             block = all_scores[part]
             if c >= prompt_len:
                 bias = live_bias[s, c - prompt_len : c - prompt_len + size, :]
                 if c + size == columns:
-                    last = bias[size - ROWS :] + causal_bias[...]
-                    bias = last if size == ROWS else jnp.concatenate([bias[: size - ROWS], last], axis=0)
+                    last = bias[size - SIDE :] + causal_bias[...]
+                    bias = last if size == SIDE else jnp.concatenate([bias[: size - SIDE], last], axis=0)
                 block = block + jnp.concatenate([bias, bias], axis=1)
             block = classes(block)
             top = jnp.max(block, axis=0) * EXP2_SCALE
@@ -286,7 +288,7 @@
         weighted = functools.reduce(jnp.add, [f * x for f, x in zip(factors, weights)])
         total = jnp.sum(total, axis=0, keepdims=True)
         weighted = jnp.sum(weighted, axis=0, keepdims=True)
-        row = index * ROWS + (lax.broadcasted_iota(jnp.int32, (1, wide), 1) & (ROWS - 1))
+        row = index * ROWS + side * SIDE + (lax.broadcasted_iota(jnp.int32, (1, wide), 1) & (SIDE - 1))
         live = (row >= begin_ref[s]) & (row < begin_ref[s] + length_ref[s])
         inverse = jnp.where(live, 1.0 / total, 0.0)
         out["delta"] = weighted * inverse
@@ -295,7 +297,7 @@
     def tail(u, side, stats):
         buf, lanes = u % 2, lanes_of(side)
         delta = stats["delta"]
-        for (c, size), factor in zip(chunks(u), stats["factors"]):
+        for (c, size), factor in zip(chunks(u, side), stats["factors"]):
             for first in range(c, c + size, PIECE):
                 part = slice(first, first + PIECE)
                 p = (classes(exps[buf, side, part, :]) * factor[None]).reshape(PIECE, wide)
@@ -303,7 +305,7 @@
                 ds = p * (dprobs[buf, side, part, :] - delta)
                 dscore16[buf, part, lanes] = ds.astype(jnp.bfloat16)
             yield
-        pad = slice(columns_of(u), padded_columns(u))
+        pad = slice(columns_of(u, side), padded_columns(u))
         if pad.start < pad.stop:
             zero = jnp.zeros((pad.stop - pad.start, wide), jnp.bfloat16)
             prob16[buf, pad, lanes] = zero
@@ -331,8 +333,8 @@
             dqt = jnp.dot(keys_t[s, :, 0:columns], ds, preferred_element_type=jnp.float32)
             dq = dqt.T * score_scale
             for h in range(at_once):
-                first = (side * at_once + h) * width
-                dq_all[rows_of(u), first : first + width] = dq[h * ROWS : (h + 1) * ROWS]
+                lanes = slice(h * width, (h + 1) * width)
+                dq_all[side_rows(u, side), lanes] = dq[h * SIDE : (h + 1) * SIDE]
             yield
 
     def together(*steps):
@@ -437,7 +439,7 @@
             pltpu.VMEM((slots, total, width), bf16),
             pltpu.VMEM((slots, width, total), bf16),
             pltpu.VMEM((slots, slot_rows, TILE), f32),
-            pltpu.VMEM((ROWS, TILE), f32),
+            pltpu.VMEM((SIDE, TILE), f32),
             pltpu.VMEM((3, 2, width, 4 * TILE), bf16),
             pltpu.VMEM((2, 2, total, 2 * TILE), f32),
             pltpu.VMEM((2, 2, total, 2 * TILE), f32),

time: 46.1 us -> 45.9 us (level)
  no operation moved by 1% of the time
where the time goes in v7:
time: 45.9 us; the launch traced here: 45.6 us
  blocking collectives  26.3 us (57%)
  Pallas kernels  12.5 us (27%)
  waiting for transfers between devices  2.94 us (6%)
  other arithmetic  1.73 us (4%)
  local copies, waits for them, and re-layouts  1.27 us (3%)
  between operations  0.65 us (1%)
    all_to_all x2, blocking collectives, exchange(): lax.all_to_all(x, 'seq', split_axis=0, concat_axis=0, axis_index_groups=s...  26.3 us
    pallas_call x1, Pallas kernels, slot_grads(): pl.pallas_call(grad_kernel, in_specs=[hbm] * 10, out_specs=[hbm] * 5, out...  12.5 us
    ppermute x2, waiting for transfers between devices, swap_cores(): return lax.ppermute(x, 'seq', [(i, i ^ 1) for i in range(n)])  2.94 us
    add x1, other arithmetic, body(): parts = exchange(own_term + swap_cores(other_term, n), n)  0.99 us
  transfers between devices with their start and end apart: 2, of which 2 were waited for; matrix products, arithmetic and copies ran while one was open for 0% of the time, Pallas kernels for 0%

profile of v7, /device:TPU:0, one launch (start us, length us, event | category | flops | bytes accessed | tf_op | source)
XLA Modules:
  0.0 45.6 jit_solution(14084887213888402733)
XLA Ops:
  0.6 0.7 %pad_add_fusion = bf16[32,256]{1,0:T(8,128)(2,1)S(1)} fusion(bf16[32,128]{1,0:T(8,128)(2,1)} %param.15, bf16[32,128]{1,0:T(8,128)(2,1)} %param.14), kind=kLoop, calls=%fused_computation | loop fusion | flops 32768 | bytes 32768 | tf_op jit(solution)/shard_map/add | solution.py:479
  1.4 14.4 %all_to_all.17 = bf16[8,32,256]{2,1,0:T(8,128)(2,1)S(1)} all-to-all(bf16[8,32,256]{2,1,0:T(8,128)(2,1)S(1)} %broadcast_in_dim.2), channel_id=1, replica_groups={{0,2,4,6,8,10,12,14},{1,3,5,7,9,11,13,15},{16,18,20,22,24,26,28,30},{17..., dimensions={0} | all-to-all | bytes 262144 | tf_op jit(solution)/shard_map/all_to_all | solution.py:33
  15.8 0.0 copy-start
  15.8 0.0 collective-permute-start
  15.8 1.3 %collective-permute-done.other_hbm = bf16[256,256]{1,0:T(8,128)(2,1)S(1)} collective-permute-done((bf16[256,256]{1,0:T(8,128)(2,1)S(1)}, bf16[256,256]{1,0:T(8,128)(2,1)S(1)}, u32[]{:S(2)}, u32[]{:S(2)}) %collective-permute-start) | collective-permute-done | bytes 131104 | tf_op jit(solution)/shard_map/ppermute | solution.py:29
  17.1 0.0 copy-done
  17.1 0.0 copy-start.1
  17.1 0.6 %copy-done.1 = bf16[256,256]{1,0:T(8,128)(2,1)} copy-done((bf16[256,256]{1,0:T(8,128)(2,1)}, bf16[256,256]{1,0:T(8,128)(2,1)S(1)}, u32[]{:S(2)}) %copy-start.1) | copy-done | bytes 131096
  17.8 12.5 %shard_map.137 = (f32[768,1024]{1,0:T(8,128)}, f32[768,128]{1,0:T(8,128)}, f32[768,128]{1,0:T(8,128)}, f32[256,256]{1,0:T(8,128)}, f32[256,256]{1,0:T(8,128)}) custom-call(s32[2]{0:T(128)} %prompt_hbm.1, s32[2]{0:T(128)} %length_hbm.1, s32[2]{0:T(128)} %begin_hbm.1, s32[16]{0:T(128)} %holder_hbm.1, bf16[768,1024]{1,0:T(8,128)(2,1)} %q_hbm.1, ...), custom_call_target="tpu_custom_call" | custom-call | tf_op jit(solution)/shard_map/pallas_call | solution.py:412
  30.3 0.2 collective-permute-start.1
  30.5 1.6 %collective-permute-done.1 = f32[256,256]{1,0:T(8,128)S(1)} collective-permute-done((f32[256,256]{1,0:T(8,128)}, f32[256,256]{1,0:T(8,128)S(1)}, u32[]{:S(2)}, u32[]{:S(2)}) %collective-permute-start.1) | collective-permute-done | bytes 262176 | tf_op jit(solution)/shard_map/ppermute | solution.py:29
  32.1 1.0 %add.11 = f32[256,256]{1,0:T(8,128)S(1)} add(f32[256,256]{1,0:T(8,128)} %get-tuple-element.13, f32[256,256]{1,0:T(8,128)S(1)} %collective-permute-done.1) | non-fusion elementwise | flops 65536 | bytes 786432 | tf_op jit(solution)/shard_map/add | solution.py:487
  33.1 11.9 %all_to_all.18 = f32[8,32,256]{2,1,0:T(8,128)S(1)} all-to-all(f32[8,32,256]{2,1,0:T(8,128)S(1)} %bitcast.2), channel_id=1, replica_groups={{0,2,4,6,8,10,12,14},{1,3,5,7,9,11,13,15},{16,18,20,22,24,26,28,30},{17..., dimensions={0} | all-to-all | bytes 524288 | tf_op jit(solution)/shard_map/all_to_all | solution.py:33
  45.0 0.6 %fusion = (f32[32,128]{1,0:T(8,128)}, f32[32,128]{1,0:T(8,128)}) fusion(f32[32,256]{1,0:T(8,128)S(1)} %reduce_sum.9), kind=kLoop, calls=%fused_computation.1 | loop fusion | bytes 65536 | tf_op jit(solution)/shard_map/slice | solution.py:489
  (2 shorter events, 0.0 us)
Async XLA Ops:
  15.8 1.4 %copy-start = (bf16[8,32,256]{2,1,0:T(8,128)(2,1)}, bf16[8,32,256]{2,1,0:T(8,128)(2,1)S(1)}, u32[]{:S(2)}) copy-start(bf16[8,32,256]{2,1,0:T(8,128)(2,1)S(1)} %all_to_all.17) | copy-start | bytes 393220
  15.8 1.3 %collective-permute-start = (bf16[256,256]{1,0:T(8,128)(2,1)S(1)}, bf16[256,256]{1,0:T(8,128)(2,1)S(1)}, u32[]{:S(2)}, u32[]{:S(2)}) collective-permute-start(bf16[256,256]{1,0:T(8,128)(2,1)S(1)} %bitcast.3), channel_id=1, source_target_pairs={{0,1},{1,0},{2,3},{3,2},{4,5},{5,4},{6,7},{7,6},{8,9},{9,8},{10,11... | collective-permute-start | bytes 393224 | tf_op jit(solution)/shard_map/ppermute | solution.py:29
  17.1 0.6 %copy-start.1 = (bf16[256,256]{1,0:T(8,128)(2,1)}, bf16[256,256]{1,0:T(8,128)(2,1)S(1)}, u32[]{:S(2)}) copy-start(bf16[256,256]{1,0:T(8,128)(2,1)S(1)} %collective-permute-done.other_hbm) | copy-start | bytes 393220
  30.3 1.8 %collective-permute-start.1 = (f32[256,256]{1,0:T(8,128)}, f32[256,256]{1,0:T(8,128)S(1)}, u32[]{:S(2)}, u32[]{:S(2)}) collective-permute-start(f32[256,256]{1,0:T(8,128)} %get-tuple-element.14), channel_id=1, source_target_pairs={{0,1},{1,0},{2,3},{3,2},{4,5},{5,4},{6,7},{7,6},{8,9},{9,8},{10,11... | collective-permute-start | bytes 786440 | tf_op jit(solution)/shard_map/ppermute | solution.py:29

commit v8 on v7

--- a/solution.py
+++ b/solution.py
@@ -326,16 +326,15 @@
         )
         yield
 
-    def flush_queries(u):
+    def flush_queries(u, side):
         s, columns = units[u][0], padded_columns(u)
-        for side in range(2):
-            ds = dscore16[u % 2, 0:columns, lanes_of(side)]
-            dqt = jnp.dot(keys_t[s, :, 0:columns], ds, preferred_element_type=jnp.float32)
-            dq = dqt.T * score_scale
-            for h in range(at_once):
-                lanes = slice(h * width, (h + 1) * width)
-                dq_all[side_rows(u, side), lanes] = dq[h * SIDE : (h + 1) * SIDE]
-            yield
+        ds = dscore16[u % 2, 0:columns, lanes_of(side)]
+        dqt = jnp.dot(keys_t[s, :, 0:columns], ds, preferred_element_type=jnp.float32)
+        dq = dqt.T * score_scale
+        for h in range(at_once):
+            lanes = slice(h * width, (h + 1) * width)
+            dq_all[side_rows(u, side), lanes] = dq[h * SIDE : (h + 1) * SIDE]
+        yield
 
     def together(*steps):
         steps = list(steps)
@@ -356,21 +355,19 @@
     count = len(units)
     per_slot = steps_of
     stats = [({}, {}) for _ in units]
+    wait_rows(0)
     together(prepare(0))
-    wait_rows(0)
     together(head(0, 0, stats[0][0]))
     for u in range(count):
         s = units[u][0]
         steps = [head(u, 1, stats[u][1]), tail(u, 0, stats[u][0])]
         if u >= 1:
-            steps += [flush_keys(u - 1), flush_queries(u - 1)]
+            steps += [flush_keys(u - 1), flush_queries(u - 1, 0)]
         if u % per_slot == 2 and s + 1 < slots:
             steps.append(prepare(s + 1))
         if u % per_slot == 1 and s >= 1:
             steps.append(finish(s - 1))
         together(*steps)
-        if u >= 1:
-            send_rows(u - 1)
         if u % per_slot == 1 and s >= 1:
             drk_copy(s - 1).start()
             drv_copy(s - 1).start()
@@ -380,11 +377,13 @@
             steps.append(head(u + 1, 0, stats[u + 1][0]))
         steps.append(tail(u, 1, stats[u][1]))
         if u >= 1:
-            steps.append(flush_values(u - 1))
+            steps += [flush_values(u - 1), flush_queries(u - 1, 1)]
         together(*steps)
-    together(flush_keys(count - 1), flush_values(count - 1), flush_queries(count - 1))
+        if u >= 1:
+            send_rows(u - 1)
+    together(flush_keys(count - 1), flush_values(count - 1))
+    together(finish(slots - 1), flush_queries(count - 1, 0), flush_queries(count - 1, 1))
     send_rows(count - 1)
-    together(finish(slots - 1))
     drk_copy(slots - 1).start()
     drv_copy(slots - 1).start()
 

time: 45.9 us -> 45.9 us (level)
  no operation moved by 1% of the time
where the time goes in v8:
time: 45.9 us; the launch traced here: 45.6 us
  blocking collectives  26.3 us (57%)
  Pallas kernels  12.4 us (27%)
  waiting for transfers between devices  2.94 us (6%)
  other arithmetic  1.73 us (4%)
  local copies, waits for them, and re-layouts  1.27 us (3%)
  between operations  0.65 us (1%)
    all_to_all x2, blocking collectives, exchange(): lax.all_to_all(x, 'seq', split_axis=0, concat_axis=0, axis_index_groups=s...  26.3 us
    pallas_call x1, Pallas kernels, slot_grads(): pl.pallas_call(grad_kernel, in_specs=[hbm] * 10, out_specs=[hbm] * 5, out...  12.4 us
    ppermute x2, waiting for transfers between devices, swap_cores(): return lax.ppermute(x, 'seq', [(i, i ^ 1) for i in range(n)])  2.94 us
    add x1, other arithmetic, body(): parts = exchange(own_term + swap_cores(other_term, n), n)  0.99 us
  transfers between devices with their start and end apart: 2, of which 2 were waited for; matrix products, arithmetic and copies ran while one was open for 0% of the time, Pallas kernels for 0%

profile of v8, /device:TPU:0, one launch (start us, length us, event | category | flops | bytes accessed | tf_op | source)
XLA Modules:
  0.0 45.6 jit_solution(1429879926460965074)
XLA Ops:
  0.6 0.7 %pad_add_fusion = bf16[32,256]{1,0:T(8,128)(2,1)S(1)} fusion(bf16[32,128]{1,0:T(8,128)(2,1)} %param.15, bf16[32,128]{1,0:T(8,128)(2,1)} %param.14), kind=kLoop, calls=%fused_computation | loop fusion | flops 32768 | bytes 32768 | tf_op jit(solution)/shard_map/add | solution.py:478
  1.4 14.4 %all_to_all.17 = bf16[8,32,256]{2,1,0:T(8,128)(2,1)S(1)} all-to-all(bf16[8,32,256]{2,1,0:T(8,128)(2,1)S(1)} %broadcast_in_dim.2), channel_id=1, replica_groups={{0,2,4,6,8,10,12,14},{1,3,5,7,9,11,13,15},{16,18,20,22,24,26,28,30},{17..., dimensions={0} | all-to-all | bytes 262144 | tf_op jit(solution)/shard_map/all_to_all | solution.py:33
  15.8 0.0 copy-start
  15.8 0.0 collective-permute-start
  15.8 1.3 %collective-permute-done.other_hbm = bf16[256,256]{1,0:T(8,128)(2,1)S(1)} collective-permute-done((bf16[256,256]{1,0:T(8,128)(2,1)S(1)}, bf16[256,256]{1,0:T(8,128)(2,1)S(1)}, u32[]{:S(2)}, u32[]{:S(2)}) %collective-permute-start) | collective-permute-done | bytes 131104 | tf_op jit(solution)/shard_map/ppermute | solution.py:29
  17.1 0.0 copy-done
  17.1 0.0 copy-start.1
  17.1 0.6 %copy-done.1 = bf16[256,256]{1,0:T(8,128)(2,1)} copy-done((bf16[256,256]{1,0:T(8,128)(2,1)}, bf16[256,256]{1,0:T(8,128)(2,1)S(1)}, u32[]{:S(2)}) %copy-start.1) | copy-done | bytes 131096
  17.8 12.4 %shard_map.137 = (f32[768,1024]{1,0:T(8,128)}, f32[768,128]{1,0:T(8,128)}, f32[768,128]{1,0:T(8,128)}, f32[256,256]{1,0:T(8,128)}, f32[256,256]{1,0:T(8,128)}) custom-call(s32[2]{0:T(128)} %prompt_hbm.1, s32[2]{0:T(128)} %length_hbm.1, s32[2]{0:T(128)} %begin_hbm.1, s32[16]{0:T(128)} %holder_hbm.1, bf16[768,1024]{1,0:T(8,128)(2,1)} %q_hbm.1, ...), custom_call_target="tpu_custom_call" | custom-call | tf_op jit(solution)/shard_map/pallas_call | solution.py:411
  30.2 0.2 collective-permute-start.1
  30.5 1.6 %collective-permute-done.1 = f32[256,256]{1,0:T(8,128)S(1)} collective-permute-done((f32[256,256]{1,0:T(8,128)}, f32[256,256]{1,0:T(8,128)S(1)}, u32[]{:S(2)}, u32[]{:S(2)}) %collective-permute-start.1) | collective-permute-done | bytes 262176 | tf_op jit(solution)/shard_map/ppermute | solution.py:29
  32.1 1.0 %add.11 = f32[256,256]{1,0:T(8,128)S(1)} add(f32[256,256]{1,0:T(8,128)} %get-tuple-element.13, f32[256,256]{1,0:T(8,128)S(1)} %collective-permute-done.1) | non-fusion elementwise | flops 65536 | bytes 786432 | tf_op jit(solution)/shard_map/add | solution.py:486
  33.0 11.9 %all_to_all.18 = f32[8,32,256]{2,1,0:T(8,128)S(1)} all-to-all(f32[8,32,256]{2,1,0:T(8,128)S(1)} %bitcast.2), channel_id=1, replica_groups={{0,2,4,6,8,10,12,14},{1,3,5,7,9,11,13,15},{16,18,20,22,24,26,28,30},{17..., dimensions={0} | all-to-all | bytes 524288 | tf_op jit(solution)/shard_map/all_to_all | solution.py:33
  45.0 0.6 %fusion = (f32[32,128]{1,0:T(8,128)}, f32[32,128]{1,0:T(8,128)}) fusion(f32[32,256]{1,0:T(8,128)S(1)} %reduce_sum.9), kind=kLoop, calls=%fused_computation.1 | loop fusion | bytes 65536 | tf_op jit(solution)/shard_map/slice | solution.py:488
  (2 shorter events, 0.0 us)
Async XLA Ops:
  15.8 1.4 %copy-start = (bf16[8,32,256]{2,1,0:T(8,128)(2,1)}, bf16[8,32,256]{2,1,0:T(8,128)(2,1)S(1)}, u32[]{:S(2)}) copy-start(bf16[8,32,256]{2,1,0:T(8,128)(2,1)S(1)} %all_to_all.17) | copy-start | bytes 393220
  15.8 1.3 %collective-permute-start = (bf16[256,256]{1,0:T(8,128)(2,1)S(1)}, bf16[256,256]{1,0:T(8,128)(2,1)S(1)}, u32[]{:S(2)}, u32[]{:S(2)}) collective-permute-start(bf16[256,256]{1,0:T(8,128)(2,1)S(1)} %bitcast.3), channel_id=1, source_target_pairs={{0,1},{1,0},{2,3},{3,2},{4,5},{5,4},{6,7},{7,6},{8,9},{9,8},{10,11... | collective-permute-start | bytes 393224 | tf_op jit(solution)/shard_map/ppermute | solution.py:29
  17.1 0.6 %copy-start.1 = (bf16[256,256]{1,0:T(8,128)(2,1)}, bf16[256,256]{1,0:T(8,128)(2,1)S(1)}, u32[]{:S(2)}) copy-start(bf16[256,256]{1,0:T(8,128)(2,1)S(1)} %collective-permute-done.other_hbm) | copy-start | bytes 393220
  30.2 1.8 %collective-permute-start.1 = (f32[256,256]{1,0:T(8,128)}, f32[256,256]{1,0:T(8,128)S(1)}, u32[]{:S(2)}, u32[]{:S(2)}) collective-permute-start(f32[256,256]{1,0:T(8,128)} %get-tuple-element.14), channel_id=1, source_target_pairs={{0,1},{1,0},{2,3},{3,2},{4,5},{5,4},{6,7},{7,6},{8,9},{9,8},{10,11... | collective-permute-start | bytes 786440 | tf_op jit(solution)/shard_map/ppermute | solution.py:29
